TPU v7x, 512 devices: a whole 4x8x8 slice. The times are simulated.
512 devices in a mesh: rep: 8 (over y_lo, core), fsdp: 64 (over y_hi, z, x).
Axes of the slice: x: 4, y: 8 (y_hi: 2, y_lo: 4; y = y_hi * 4 + y_lo), z: 8, core: 2. Of those that a mesh axis runs over, the one named last changes fastest.
Arguments:
- grad_parts: bfloat16 [8, 64, 128, 6144], P('rep', 'fsdp'), may hold values from -6 to 6
- master: float32 [8, 128, 6144], P('rep', None, 'fsdp'), may hold values from -6 to 6
- moment1: float32 [8, 128, 6144], P('rep', None, 'fsdp'), may hold values from -6 to 6
- moment2: float32 [8, 128, 6144], P('rep', None, 'fsdp'), may hold values from 0.1 to 4
- probe: float32 [6144], P('fsdp'), may hold values from -0.078125 to 0.078125
- flagged: int32 [8], replicated, may hold values from 0 to 511, as said below
- source: int32 [8], replicated, may hold values from 0 to 7, as said below
- step_count: int32 [1], replicated, may hold values from 1 to 11
Outputs:
- new_master: float32 [8, 128, 6144], P('rep', None, 'fsdp')
- new_moment1: float32 [8, 128, 6144], P('rep', None, 'fsdp')
- new_moment2: float32 [8, 128, 6144], P('rep', None, 'fsdp')
- params: bfloat16 [8, 128, 6144], P('rep', None, 'fsdp')
- checksum: float32 [8, 128], P('rep')
Inputs may be any that keep to these rules, and one draw needn't show every extreme that they name: `flagged`: 8 devices, no two with the same shard. source[k] differs from flagged[k] // 64.
All inputs are finite; a program needn't handle non-finite values.
Results may differ from a plain program's by a relative error of at most 0.001.
Values sent between devices are 32-bit elements; how exact they have to be, the bound alone decides.
No kernel may reach another device: no remote copies, remote signals or barrier semaphores. Data moves between devices by JAX's collectives and lax.ppermute only.
A program may use at most 64 MiB of HBM per device.

v0:
```python
import jax
import jax.numpy as jnp
from jax import lax
from jax.sharding import PartitionSpec as P

beta_one = 0.9
beta_two = 0.95
learn_rate = 0.05
decay_rate = 0.1
epsilon = 1e-08


def from_root(value, axis, source):
    kept = jnp.where(lax.axis_index(axis) == source, value, 0).astype(value.dtype)
    return lax.psum(kept, axis)


def adamw_update(master, first, second, grad, step_count):
    new_first = beta_one * first + (1.0 - beta_one) * grad[None]
    new_second = beta_two * second + (1.0 - beta_two) * (grad * grad)[None]
    steps_done = step_count[0].astype(jnp.float32)
    correct_one = 1.0 - jnp.power(jnp.float32(beta_one), steps_done)
    correct_two = 1.0 - jnp.power(jnp.float32(beta_two), steps_done)
    update = new_first / correct_one / (jnp.sqrt(new_second / correct_two) + epsilon)
    new_master = master - learn_rate * (update + decay_rate * master)
    return (new_master, new_first, new_second)


def shards(grad_parts, master, moment1, moment2, probe, flagged, source, step_count):
    partial_grad = grad_parts[0, 0].astype(jnp.float32)
    grad_shard = lax.psum_scatter(partial_grad, "fsdp", scatter_dimension=1, tiled=True)
    grad = lax.psum(grad_shard, "rep")
    shard_count = lax.axis_size("fsdp")
    my_replica = lax.axis_index("rep")
    my_shard = lax.axis_index("fsdp")
    flagged_here = jnp.any(flagged == my_replica * shard_count + my_shard)
    shard_match = flagged % shard_count == my_shard
    donor_index = jnp.sum(jnp.where(shard_match, source, 0))
    donor = (
        from_root(master, "rep", donor_index),
        from_root(moment1, "rep", donor_index),
        from_root(moment2, "rep", donor_index),
    )
    healed_master = jnp.where(flagged_here, donor[0], master)
    healed_first = jnp.where(flagged_here, donor[1], moment1)
    healed_second = jnp.where(flagged_here, donor[2], moment2)
    new_master, new_first, new_second = adamw_update(
        healed_master, healed_first, healed_second, grad, step_count
    )
    params = new_master.astype(jnp.bfloat16)
    local_sums = jnp.sum(new_master[0] * probe[None, :], axis=1)
    checksum = lax.psum(local_sums, "fsdp")
    return (new_master, new_first, new_second, params, checksum.reshape(1, -1))


def solution(mesh):
    placed = (
        P("rep", "fsdp", None, None),
        P("rep", None, "fsdp"),
        P("rep", None, "fsdp"),
        P("rep", None, "fsdp"),
        P("fsdp"),
        P(),
        P(),
        P(),
    )
    return jax.shard_map(
        shards,
        mesh=mesh,
        in_specs=placed,
        out_specs=(
            P("rep", None, "fsdp"),
            P("rep", None, "fsdp"),
            P("rep", None, "fsdp"),
            P("rep", None, "fsdp"),
            P("rep", None),
        ),
        check_vma=False,
    )
```

profile of v0, /device:TPU:32, one launch (start us, length us, event | category | flops | bytes accessed | tf_op | source)
XLA Modules:
  0.0 1156.7 jit_solution(10767033278393999551)
XLA Ops:
  7.2 0.0 reduce-scatter.2.cloned.1.call-start
  7.2 1.9 copy.13
  9.1 1.9 bitcast_convert_fusion
  11.0 0.0 copy-start.5
  11.0 0.0 copy-start.6
  11.0 0.0 copy-start
  11.0 0.0 copy-start.2
  11.0 0.0 copy-start.3
  11.0 0.0 copy-start.4
  11.0 0.0 reduce-scatter.2.cloned.1.call-update
  11.1 0.0 all-reduce.3.cloned.1.call-start
  11.1 0.5 copy-done.5
  11.7 0.0 copy-done.6
  11.7 0.6 fusion.2
  13.0 0.0 copy-done
  13.0 0.6 broadcast_select_fusion.2
  13.6 0.0 copy-done.2
  13.6 0.0 copy-done.3
  13.6 0.6 broadcast_select_fusion
  14.3 834.0 %reduce-scatter.2.cloned.1.call-done = f32[128,96]{0,1:T(8,128)} async-done(((f32[128,6144]{0,1:T(8,128)}), f32[128,96]{0,1:T(8,128)}) %reduce-scatter.2.cloned.1.call-update) | async-done | bytes 49168 | tf_op jit(solution)/shard_map/reduce_scatter | solution.py:31
  848.3 0.0 all-reduce.3.cloned.1.call-update
  849.0 0.7 compare_reduce_fusion
  849.7 73.9 %all-reduce.3.cloned.1.call-done = (f32[128,96]{0,1:T(8,128)}, f32[1,128,96]{1,2,0:T(8,128)}, f32[1,128,96]{1,2,0:T(8,128)}, f32[1,128,96]{1,2,0:T(8,128)}) async-done(((f32[128,96]{0,1:T(8,128)}, f32[1,128,96]{1,2,0:T(8,128)}, f32[1,128,96]{1,2,0:T(8,128)}, f32[1,128,96]{1,2,0:T(8,128)}), (f32[128,96]{0,1:T(8,128)}, f32[1,128,96]{1,2,0:T(8,128)}, f32[1,128,96]{1,2,0:T(8,128)}, ...) | async-done | bytes 196624 | tf_op jit(solution)/shard_map/psum | solution.py:32
  923.6 0.0 copy-done.4
  923.6 2.1 fusion
  925.7 0.0 copy-start.1
  925.7 0.6 convert_element_type.20
  926.3 223.5 %psum.39 = f32[1,128]{1,0:T(1,128)} all-reduce(f32[1,128]{1,0:T(1,128)S(1)} %bitcast.16), channel_id=1, replica_groups=mesh['rep'=8,'fsdp'=64] {'fsdp'}, use_global_device_ids=true, to_apply=%region_8.9 | all-reduce | flops 128 | bytes 1024 | tf_op jit(solution)/shard_map/psum | solution.py:52
  1149.8 0.0 copy-done.1
Async XLA Ops:
  7.2 841.1 %reduce-scatter.2.cloned.1.call-start = ((), (), s32[]{:S(2)}) async-start(), calls=%async_computation.1 | async-start | bytes 3194880 | tf_op jit(solution)/shard_map/reduce_scatter | solution.py:31
  11.0 0.7 copy-start.5
  11.0 0.7 copy-start.6
  11.0 2.0 copy-start
  11.0 2.6 copy-start.2
  11.0 2.6 copy-start.3
  11.0 912.6 %copy-start.4 = (f32[96]{0:T(128)S(1)}, f32[96]{0:T(128)}, u32[]{:S(2)}) copy-start(f32[96]{0:T(128)} %param.12) | copy-start | bytes 1156
  11.1 912.5 %all-reduce.3.cloned.1.call-start = ((), (), s32[]{:S(2)}) async-start(), calls=%async_computation.2 | async-start | bytes 393216 | tf_op jit(solution)/shard_map/psum | solution.py:32
  925.7 224.1 %copy-start.1 = (f32[1,128,96]{1,2,0:T(8,128)}, f32[1,128,96]{1,2,0:T(8,128)S(1)}, u32[]{:S(2)}) copy-start(f32[1,128,96]{1,2,0:T(8,128)S(1)} %get-tuple-element.10) | copy-start | bytes 147460
Sparse Core Ops, SparseCore 0:
  14.4 833.8 reduce-scatter.1
  852.3 71.2 all-reduce.2
where the time goes:
time: 1160 us
  waiting for transfers between devices  908 us (78%)
  blocking collectives  223 us (19%)
  between operations  15.5 us (1%)
    reduce_scatter x1, waiting for transfers between devices, shards(): lax.psum_scatter(partial_grad, 'fsdp', scatter_dimension=1, tiled=True)  834 us
    psum x1, blocking collectives, shards(): checksum = lax.psum(local_sums, 'fsdp')  223 us
    psum x1, waiting for transfers between devices, shards(): grad = lax.psum(grad_shard, 'rep')  73.9 us
  transfers between devices with their start and end apart: 2, of which 2 were waited for; matrix products, arithmetic and copies ran while one was open for 0% of the time, Pallas kernels for 0%

commit v1 on v0

v1 whole, which is shorter than its diff:
```python
import jax
import jax.numpy as jnp
from jax import lax
from jax.sharding import Mesh, PartitionSpec as P

beta_one = 0.9
beta_two = 0.95
learn_rate = 0.05
decay_rate = 0.1
epsilon = 1e-08

YL, C, YH, Z, X = 4, 2, 2, 8, 4
REP = ("yl", "c")
FSDP = ("yh", "z", "x")
WIDTH, HALF, FEAT = 96, 48, 128


def swapped(value, axis, size, bit):
    return lax.ppermute(value, axis, [(i, i ^ bit) for i in range(size)])


def adamw_update(master, first, second, grad, step_count):
    new_first = beta_one * first + (1.0 - beta_one) * grad
    new_second = beta_two * second + (1.0 - beta_two) * (grad * grad)
    steps_done = step_count[0].astype(jnp.float32)
    correct_one = 1.0 - jnp.power(jnp.float32(beta_one), steps_done)
    correct_two = 1.0 - jnp.power(jnp.float32(beta_two), steps_done)
    update = new_first / correct_one / (jnp.sqrt(new_second / correct_two) + epsilon)
    new_master = master - learn_rate * (update + decay_rate * master)
    return (new_master, new_first, new_second)


def reduced_grad(grad_parts):
    core = lax.axis_index("c")
    columns = grad_parts[0, 0].T.astype(jnp.float32)
    columns = columns.reshape(YH, Z, X, C, HALF, FEAT).transpose(3, 1, 2, 0, 4, 5)
    kept = jnp.where(core == 0, columns[0], columns[1])
    given = jnp.where(core == 0, columns[1], columns[0])
    chip = kept + swapped(given, "c", C, 1)
    blocks = lax.all_to_all(chip.reshape(Z * X, YH * HALF, FEAT), ("z", "x"), 0, 0, tiled=True)
    plane = jnp.sum(blocks, axis=0).reshape(YH, 1, HALF, FEAT)
    spread = jnp.broadcast_to(plane, (YH, YL, HALF, FEAT)).reshape(YH * YL, HALF, FEAT)
    lines = lax.all_to_all(spread, ("yh", "yl"), 0, 0, tiled=True)
    half = jnp.sum(lines, axis=0)
    return lax.all_gather(half, "c", axis=0, tiled=True)


def healed_state(state, flagged, source):
    my_replica = lax.axis_index(REP)
    my_shard = lax.axis_index(FSDP)
    match = flagged % (YH * Z * X) == my_shard
    replica = flagged // (YH * Z * X)
    step = jnp.sum(jnp.where(match, replica ^ source, 0))
    flagged_here = jnp.any(match & (replica == my_replica))
    moved = state
    for axis, size, bit, place in (("c", C, 1, 1), ("yl", YL, 1, 2), ("yl", YL, 2, 4)):
        other = swapped(moved, axis, size, bit)
        moved = jnp.where((step & place) != 0, other, moved)
    return jnp.where(flagged_here, moved, state)


def shards(grad_parts, master, moment1, moment2, probe, flagged, source, step_count):
    grad = reduced_grad(grad_parts)
    state = jnp.stack([master[0].T, moment1[0].T, moment2[0].T])
    healed = healed_state(state, flagged, source)
    new_master, new_first, new_second = adamw_update(
        healed[0], healed[1], healed[2], grad, step_count
    )
    local_sums = jnp.sum(new_master * probe[:, None], axis=0)
    spread = jnp.broadcast_to(local_sums, (Z * X, FEAT))
    plane_sums = jnp.sum(lax.all_to_all(spread, ("z", "x"), 0, 0, tiled=True), axis=0)
    checksum = plane_sums + swapped(plane_sums, "yh", YH, 1)
    params = new_master.astype(jnp.bfloat16)
    return (
        new_master.T[None],
        new_first.T[None],
        new_second.T[None],
        params.T[None],
        checksum.reshape(1, -1),
    )


def solution(mesh):
    named = Mesh(mesh.devices.reshape(YL, C, YH, Z, X), REP + FSDP)
    state = P(REP, None, FSDP)
    placed = (P(REP, FSDP, None, None), state, state, state, P(FSDP), P(), P(), P())
    return jax.shard_map(
        shards,
        mesh=named,
        in_specs=placed,
        out_specs=(state, state, state, state, P(REP, None)),
        check_vma=False,
    )
```

time: 1160 us -> 110 us (0.09)
  the two profiles are of different devices: /device:TPU:32 before, /device:TPU:1 now
where the time goes in v1:
time: 110 us; the launch traced here: 109 us
  waiting for transfers between devices  40.1 us (36%)
  starting transfers between devices  35.4 us (32%)
  blocking collectives  19 us (17%)
  other arithmetic  6.13 us (6%)
  local copies, waits for them, and re-layouts  4.68 us (4%)
  between operations  3.51 us (3%)
    all_to_all x1, waiting for transfers between devices, reduced_grad(): lax.all_to_all(chip.reshape(Z * X, YH * HALF, FEAT), ('z', 'x'), 0, 0, ti...  21.5 us
    ppermute x5, starting transfers between devices, swapped(): return lax.ppermute(value, axis, [(i, i ^ bit) for i in range(size)])  21 us
    all_to_all x1, blocking collectives, shards(): lax.all_to_all(spread, ('z', 'x'), 0, 0, tiled=True)  13.9 us
    ppermute x5, waiting for transfers between devices, swapped(): return lax.ppermute(value, axis, [(i, i ^ bit) for i in range(size)])  11.9 us
    all_to_all x1, starting transfers between devices, reduced_grad(): lax.all_to_all(chip.reshape(Z * X, YH * HALF, FEAT), ('z', 'x'), 0, 0, ti...  7.65 us
    all_to_all x1, starting transfers between devices, reduced_grad(): lines = lax.all_to_all(spread, ('yh', 'yl'), 0, 0, tiled=True)  6.82 us
    all_to_all x1, waiting for transfers between devices, reduced_grad(): lines = lax.all_to_all(spread, ('yh', 'yl'), 0, 0, tiled=True)  6.66 us
    all_gather x1, blocking collectives, reduced_grad(): return lax.all_gather(half, 'c', axis=0, tiled=True)  5.14 us
  transfers between devices with their start and end apart: 7, of which 5 were waited for; matrix products, arithmetic and copies ran while one was open for 3% of the time, Pallas kernels for 0%

profile of v1, /device:TPU:1, one launch (start us, length us, event | category | flops | bytes accessed | tf_op | source)
XLA Modules:
  0.0 108.8 jit_solution(14636039335050007569)
XLA Ops:
  0.6 2.6 %copy.29 = bf16[1,1,128,6144]{2,3,1,0:T(8,128)(2,1)} copy(bf16[1,1,128,6144]{3,2,1,0:T(8,128)(2,1)} %param.8) | data formatting | bytes 3145728 | tf_op args[0]
  3.2 1.6 %bitcast_convert_fusion = f32[128,6144]{0,1:T(8,128)S(1)} fusion(bf16[1,1,128,6144]{2,3,1,0:T(8,128)(2,1)} %copy.29), kind=kLoop, calls=%fused_computation.3 | loop fusion | flops 786432 | bytes 4718592 | tf_op jit(solution)/shard_map/transpose | solution.py:36
  4.9 0.2 select_bitcast_fusion
  5.1 8.8 %collective-permute-start.3 = (f32[8,4,2,48,128]{4,3,1,0,2:T(8,128)S(1)}, f32[8,4,2,48,128]{4,3,1,0,2:T(8,128)S(1)}, u32[]{:S(2)}, u32[]{:S(2)}) collective-permute-start(f32[8,4,2,48,128]{4,3,1,0,2:T(8,128)S(1)} %select_bitcast_fusion), channel_id=1, source_target_pairs={{0,64},{64,0},{1,65},{65,1},{2,66},{66,2},{3,67},{67,3},{4,68},{68... | collective-permute-start | bytes 4718600 | tf_op jit(solution)/shard_map/ppermute | solution.py:19
  13.8 3.0 %collective-permute-done.3 = f32[8,4,2,48,128]{4,3,1,0,2:T(8,128)S(1)} collective-permute-done((f32[8,4,2,48,128]{4,3,1,0,2:T(8,128)S(1)}, f32[8,4,2,48,128]{4,3,1,0,2:T(8,128)S(1)}, u32[]{:S(2)}, u32[]{:S(2)}) %collective-permute-start.3) | collective-permute-done | bytes 1572896 | tf_op jit(solution)/shard_map/ppermute | solution.py:19
  16.9 0.4 fusion.1
  17.3 1.4 %copy.34 = f32[8,4,2,48,128]{4,3,2,1,0:T(8,128)} copy(f32[8,4,2,48,128]{4,3,1,0,2:T(8,128)S(1)} %fusion.1) | data formatting | bytes 3145728 | tf_op jit(solution)/shard_map/add | solution.py:39
  18.6 0.0 copy-start.6
  18.7 7.7 %all-to-all-start = ((f32[32,96,128]{2,1,0:T(8,128)}), f32[32,96,128]{2,1,0:T(8,128)S(1)}, u32[]{:S(2)}, u32[]{:S(2)}) async-start(f32[32,96,128]{2,1,0:T(8,128)} %bitcast.23), calls=%async_computation | async-start | bytes 3145728 | tf_op jit(solution)/shard_map/all_to_all | solution.py:40
  26.3 0.0 copy-done
  26.4 2.6 %collective-permute-start = (f32[3,96,128]{2,1,0:T(8,128)S(1)}, f32[3,96,128]{2,1,0:T(8,128)S(1)}, u32[]{:S(2)}, u32[]{:S(2)}) collective-permute-start(f32[3,96,128]{2,1,0:T(8,128)S(1)} %pad_maximum_fusion), channel_id=1, source_target_pairs={{0,64},{64,0},{1,65},{65,1},{2,66},{66,2},{3,67},{67,3},{4,68},{68... | collective-permute-start | bytes 442376 | tf_op jit(solution)/shard_map/ppermute | solution.py:19
  29.0 0.6 and_reduce_fusion
  29.6 0.6 fusion.8
  30.9 0.0 collective-permute-done
  30.9 3.2 %collective-permute-start.1 = (f32[3,96,128]{2,1,0:T(8,128)S(1)}, f32[3,96,128]{2,1,0:T(8,128)S(1)}, u32[]{:S(2)}, u32[]{:S(2)}) collective-permute-start(f32[3,96,128]{2,1,0:T(8,128)S(1)} %broadcast_select_fusion), channel_id=1, source_target_pairs={{0,128},{128,0},{256,384},{384,256},{1,129},{129,1},{257,385},{385... | collective-permute-start | bytes 442376 | tf_op jit(solution)/shard_map/ppermute | solution.py:19
  34.8 3.5 %collective-permute-done.1 = f32[3,96,128]{2,1,0:T(8,128)S(1)} collective-permute-done((f32[3,96,128]{2,1,0:T(8,128)S(1)}, f32[3,96,128]{2,1,0:T(8,128)S(1)}, u32[]{:S(2)}, u32[]{:S(2)}) %collective-permute-start.1) | collective-permute-done | bytes 147488 | tf_op jit(solution)/shard_map/ppermute | solution.py:19
  38.3 0.0 copy-start.5
  38.3 4.2 %collective-permute-start.2 = (f32[3,96,128]{2,1,0:T(8,128)S(1)}, f32[3,96,128]{2,1,0:T(8,128)S(1)}, u32[]{:S(2)}, u32[]{:S(2)}) collective-permute-start(f32[3,96,128]{2,1,0:T(8,128)S(1)} %broadcast_select_fusion.1), channel_id=1, source_target_pairs={{0,256},{128,384},{256,0},{384,128},{1,257},{129,385},{257,1},{385... | collective-permute-start | bytes 442376 | tf_op jit(solution)/shard_map/ppermute | solution.py:19
  42.6 21.5 %all-to-all-done = f32[32,96,128]{2,1,0:T(8,128)S(1)} async-done(((f32[32,96,128]{2,1,0:T(8,128)}), f32[32,96,128]{2,1,0:T(8,128)S(1)}, u32[]{:S(2)}, u32[]{:S(2)}) %all-to-all-start) | async-done | bytes 1572896 | tf_op jit(solution)/shard_map/all_to_all | solution.py:40
  64.1 0.1 reduce_sum.46
  64.2 0.7 broadcast_in_dim.26
  64.8 6.8 %all-to-all-start.1 = ((f32[8,48,128]{2,1,0:T(8,128)}), f32[8,48,128]{2,1,0:T(8,128)S(1)}, u32[]{:S(2)}, u32[]{:S(2)}) async-start(f32[8,48,128]{2,1,0:T(8,128)} %bitcast.25), calls=%async_computation.1 | async-start | bytes 393216 | tf_op jit(solution)/shard_map/all_to_all | solution.py:43
  73.0 0.0 collective-permute-done.2
  73.1 0.7 select_select_fusion
  73.7 6.7 %all-to-all-done.1 = f32[8,48,128]{2,1,0:T(8,128)S(1)} async-done(((f32[8,48,128]{2,1,0:T(8,128)}), f32[8,48,128]{2,1,0:T(8,128)S(1)}, u32[]{:S(2)}, u32[]{:S(2)}) %all-to-all-start.1) | async-done | bytes 196640 | tf_op jit(solution)/shard_map/all_to_all | solution.py:43
  80.4 5.1 %all_gather.3 = f32[96,128]{1,0:T(8,128)S(1)} all-gather(f32[48,128]{1,0:T(8,128)S(1)} %reduce_sum.47), channel_id=1, replica_groups=mesh['yl'=4,'c'=2,'yh'=2,'z'=8,'x'=4] {'c'}, dimensions={0}, use_global_device_ids=true | all-gather | bytes 73728 | tf_op jit(solution)/shard_map/all_gather | solution.py:45
  85.6 0.7 fusion.7
  86.2 13.9 %all_to_all.16 = f32[32,1,128]{2,1,0:T(1,128)S(1)} all-to-all(f32[32,1,128]{2,1,0:T(1,128)S(1)} %broadcast_in_dim.31), channel_id=1, replica_groups=mesh['yl'=4,'c'=2,'yh'=2,'z'=8,'x'=4] {'z','x'}, dimensions={0} | all-to-all | bytes 32768 | tf_op jit(solution)/shard_map/all_to_all | solution.py:71
  100.1 2.2 %collective-permute-start.4 = (f32[128]{0:T(128)S(1)}, f32[128]{0:T(128)S(1)}, u32[]{:S(2)}, u32[]{:S(2)}) collective-permute-start(f32[128]{0:T(128)S(1)} %reduce_sum.49), channel_id=1, source_target_pairs={{0,32},{32,0},{1,33},{33,1},{2,34},{34,2},{3,35},{35,3},{4,36},{36... | collective-permute-start | bytes 1544 | tf_op jit(solution)/shard_map/ppermute | solution.py:19
  102.3 0.6 convert_bitcast_fusion
  102.9 5.4 %collective-permute-done.4 = f32[128]{0:T(128)S(1)} collective-permute-done((f32[128]{0:T(128)S(1)}, f32[128]{0:T(128)S(1)}, u32[]{:S(2)}, u32[]{:S(2)}) %collective-permute-start.4) | collective-permute-done | bytes 544 | tf_op jit(solution)/shard_map/ppermute | solution.py:19
  108.3 0.5 add_bitcast_fusion
  (17 shorter events, 0.1 us)
Async XLA Ops:
  5.1 11.8 %collective-permute-start.3 = (f32[8,4,2,48,128]{4,3,1,0,2:T(8,128)S(1)}, f32[8,4,2,48,128]{4,3,1,0,2:T(8,128)S(1)}, u32[]{:S(2)}, u32[]{:S(2)}) collective-permute-start(f32[8,4,2,48,128]{4,3,1,0,2:T(8,128)S(1)} %select_bitcast_fusion), channel_id=1, source_target_pairs={{0,64},{64,0},{1,65},{65,1},{2,66},{66,2},{3,67},{67,3},{4,68},{68... | collective-permute-start | bytes 4718600 | tf_op jit(solution)/shard_map/ppermute | solution.py:19
  18.6 7.7 %copy-start = (f32[1,128,96]{1,2,0:T(8,128)S(1)}, f32[1,128,96]{1,2,0:T(8,128)}, u32[]{:S(2)}) copy-start(f32[1,128,96]{1,2,0:T(8,128)} %param.11) | copy-start | bytes 147460
  18.6 7.7 %copy-start.1 = (f32[1,128,96]{1,2,0:T(8,128)S(1)}, f32[1,128,96]{1,2,0:T(8,128)}, u32[]{:S(2)}) copy-start(f32[1,128,96]{1,2,0:T(8,128)} %param.10) | copy-start | bytes 147460
  18.6 7.7 %copy-start.2 = (f32[1,128,96]{1,2,0:T(8,128)S(1)}, f32[1,128,96]{1,2,0:T(8,128)}, u32[]{:S(2)}) copy-start(f32[1,128,96]{1,2,0:T(8,128)} %param.9) | copy-start | bytes 147460
  18.6 10.3 %copy-start.4 = (s32[8]{0:T(128)S(1)}, s32[8]{0:T(128)}, u32[]{:S(2)}) copy-start(s32[8]{0:T(128)} %param.13) | copy-start | bytes 100
  18.6 11.0 %copy-start.6 = (s32[8]{0:T(128)S(1)}, s32[8]{0:T(128)}, u32[]{:S(2)}) copy-start(s32[8]{0:T(128)} %param.14) | copy-start | bytes 100
  18.7 45.4 %all-to-all-start = ((f32[32,96,128]{2,1,0:T(8,128)}), f32[32,96,128]{2,1,0:T(8,128)S(1)}, u32[]{:S(2)}, u32[]{:S(2)}) async-start(f32[32,96,128]{2,1,0:T(8,128)} %bitcast.23), calls=%async_computation | async-start | bytes 3145728 | tf_op jit(solution)/shard_map/all_to_all | solution.py:40
  26.4 4.5 %collective-permute-start = (f32[3,96,128]{2,1,0:T(8,128)S(1)}, f32[3,96,128]{2,1,0:T(8,128)S(1)}, u32[]{:S(2)}, u32[]{:S(2)}) collective-permute-start(f32[3,96,128]{2,1,0:T(8,128)S(1)} %pad_maximum_fusion), channel_id=1, source_target_pairs={{0,64},{64,0},{1,65},{65,1},{2,66},{66,2},{3,67},{67,3},{4,68},{68... | collective-permute-start | bytes 442376 | tf_op jit(solution)/shard_map/ppermute | solution.py:19
  30.9 7.4 %collective-permute-start.1 = (f32[3,96,128]{2,1,0:T(8,128)S(1)}, f32[3,96,128]{2,1,0:T(8,128)S(1)}, u32[]{:S(2)}, u32[]{:S(2)}) collective-permute-start(f32[3,96,128]{2,1,0:T(8,128)S(1)} %broadcast_select_fusion), channel_id=1, source_target_pairs={{0,128},{128,0},{256,384},{384,256},{1,129},{129,1},{257,385},{385... | collective-permute-start | bytes 442376 | tf_op jit(solution)/shard_map/ppermute | solution.py:19
  38.3 47.2 %copy-start.5 = (f32[96]{0:T(128)S(1)}, f32[96]{0:T(128)}, u32[]{:S(2)}) copy-start(f32[96]{0:T(128)} %param.12) | copy-start | bytes 1156
  38.3 34.7 %collective-permute-start.2 = (f32[3,96,128]{2,1,0:T(8,128)S(1)}, f32[3,96,128]{2,1,0:T(8,128)S(1)}, u32[]{:S(2)}, u32[]{:S(2)}) collective-permute-start(f32[3,96,128]{2,1,0:T(8,128)S(1)} %broadcast_select_fusion.1), channel_id=1, source_target_pairs={{0,256},{128,384},{256,0},{384,128},{1,257},{129,385},{257,1},{385... | collective-permute-start | bytes 442376 | tf_op jit(solution)/shard_map/ppermute | solution.py:19
  64.8 15.6 %all-to-all-start.1 = ((f32[8,48,128]{2,1,0:T(8,128)}), f32[8,48,128]{2,1,0:T(8,128)S(1)}, u32[]{:S(2)}, u32[]{:S(2)}) async-start(f32[8,48,128]{2,1,0:T(8,128)} %bitcast.25), calls=%async_computation.1 | async-start | bytes 393216 | tf_op jit(solution)/shard_map/all_to_all | solution.py:43
  86.2 22.6 %copy-start.3 = (f32[96,128]{1,0:T(8,128)}, f32[96,128]{1,0:T(8,128)S(1)}, u32[]{:S(2)}) copy-start(f32[96,128]{1,0:T(8,128)S(1)} %get-tuple-element.12) | copy-start | bytes 147460
  100.1 8.2 %collective-permute-start.4 = (f32[128]{0:T(128)S(1)}, f32[128]{0:T(128)S(1)}, u32[]{:S(2)}, u32[]{:S(2)}) collective-permute-start(f32[128]{0:T(128)S(1)} %reduce_sum.49), channel_id=1, source_target_pairs={{0,32},{32,0},{1,33},{33,1},{2,34},{34,2},{3,35},{35,3},{4,36},{36... | collective-permute-start | bytes 1544 | tf_op jit(solution)/shard_map/ppermute | solution.py:19

commit v2 on v1

--- a/solution.py
+++ b/solution.py
@@ -1,6 +1,8 @@
 import jax
 import jax.numpy as jnp
 from jax import lax
+from jax.experimental import pallas as pl
+from jax.experimental.pallas import tpu as pltpu
 from jax.sharding import Mesh, PartitionSpec as P
 
 beta_one = 0.9
@@ -12,7 +14,8 @@
 YL, C, YH, Z, X = 4, 2, 2, 8, 4
 REP = ("yl", "c")
 FSDP = ("yh", "z", "x")
-WIDTH, HALF, FEAT = 96, 48, 128
+WIDTH, HALF, FEAT = 96, 64, 128
+TURN_STEPS = 8
 
 
 def swapped(value, axis, size, bit):
@@ -30,19 +33,47 @@
     return (new_master, new_first, new_second)
 
 
-def reduced_grad(grad_parts):
+def turn_kernel(half_ref, grad_ref, turned_ref):
+    columns = Z * X * WIDTH
+    wide = columns // TURN_STEPS
+    for i in range(TURN_STEPS):
+        first = grad_ref[:, i * wide : (i + 1) * wide]
+        second = grad_ref[:, columns + i * wide : columns + (i + 1) * wide]
+        both = jnp.concatenate([first, second], axis=0)
+        turned_ref[i * wide : (i + 1) * wide, :] = both.T.astype(jnp.float32)
+
+
+def turned(grad, half):
+    columns = Z * X * WIDTH
+    return pl.pallas_call(
+        turn_kernel,
+        grid_spec=pltpu.PrefetchScalarGridSpec(
+            num_scalar_prefetch=1,
+            grid=(1,),
+            in_specs=[pl.BlockSpec((HALF, YH * columns), lambda i, half_ref: (half_ref[0], 0))],
+            out_specs=pl.BlockSpec(memory_space=pltpu.VMEM),
+        ),
+        out_shape=pltpu.VMEM((columns, FEAT), jnp.float32),
+        cost_estimate=pl.CostEstimate(flops=0, bytes_accessed=columns * FEAT * 6, transcendentals=0),
+    )(half.reshape(1), grad)
+
+
+def chip_sum(grad_parts, beside):
     core = lax.axis_index("c")
-    columns = grad_parts[0, 0].T.astype(jnp.float32)
-    columns = columns.reshape(YH, Z, X, C, HALF, FEAT).transpose(3, 1, 2, 0, 4, 5)
-    kept = jnp.where(core == 0, columns[0], columns[1])
-    given = jnp.where(core == 0, columns[1], columns[0])
-    chip = kept + swapped(given, "c", C, 1)
-    blocks = lax.all_to_all(chip.reshape(Z * X, YH * HALF, FEAT), ("z", "x"), 0, 0, tiled=True)
-    plane = jnp.sum(blocks, axis=0).reshape(YH, 1, HALF, FEAT)
-    spread = jnp.broadcast_to(plane, (YH, YL, HALF, FEAT)).reshape(YH * YL, HALF, FEAT)
+    grad = grad_parts[0, 0]
+    given = swapped(turned(grad, 1 - core), "c", C, 1)
+    kept, beside = lax.optimization_barrier((turned(grad, core), beside))
+    return kept + given, beside
+
+
+def reduced_grad(chip, beside):
+    blocks = lax.all_to_all(chip.reshape(Z * X, WIDTH, FEAT), ("z", "x"), 0, 0, tiled=True)
+    plane = jnp.sum(blocks, axis=0)
+    plane, beside = lax.optimization_barrier((plane, beside))
+    spread = jnp.broadcast_to(plane, (YH * YL, WIDTH, FEAT))
     lines = lax.all_to_all(spread, ("yh", "yl"), 0, 0, tiled=True)
-    half = jnp.sum(lines, axis=0)
-    return lax.all_gather(half, "c", axis=0, tiled=True)
+    line = jnp.sum(lines, axis=0)
+    return lax.all_gather(line, "c", axis=0, tiled=False), beside
 
 
 def healed_state(state, flagged, source):
@@ -60,16 +91,37 @@
 
 
 def shards(grad_parts, master, moment1, moment2, probe, flagged, source, step_count):
-    grad = reduced_grad(grad_parts)
-    state = jnp.stack([master[0].T, moment1[0].T, moment2[0].T])
+    my_half = lax.axis_index("yh")
+    chip, state = chip_sum(grad_parts, (master[0].T, moment1[0].T, moment2[0].T))
+    state = jnp.stack(state).reshape(3 * WIDTH, FEAT)
     healed = healed_state(state, flagged, source)
-    new_master, new_first, new_second = adamw_update(
-        healed[0], healed[1], healed[2], grad, step_count
+    weights = jnp.pad(jnp.broadcast_to(probe, (8, WIDTH)), ((0, 0), (0, FEAT - WIDTH)))
+    mine = jnp.concatenate([healed, weights])
+    other = swapped(mine, "yh", YH, 1)
+    low, high = jnp.where(my_half == 0, mine, other), jnp.where(my_half == 0, other, mine)
+    packed = jnp.stack(
+        [
+            jnp.concatenate([low[: 3 * WIDTH, :HALF], high[: 3 * WIDTH, :HALF]], axis=1),
+            jnp.concatenate([low[: 3 * WIDTH, HALF:], high[: 3 * WIDTH, HALF:]], axis=1),
+        ]
     )
-    local_sums = jnp.sum(new_master * probe[:, None], axis=0)
+    first_lanes = lax.broadcasted_iota(jnp.int32, (WIDTH, FEAT), 1) < HALF
+    weights = jnp.where(
+        first_lanes, low[3 * WIDTH, :WIDTH, None], high[3 * WIDTH, :WIDTH, None]
+    )
+    grad, (packed, weights) = reduced_grad(chip, (packed, weights))
+    states = packed.reshape(C, 3, WIDTH, FEAT)
+    news = adamw_update(states[:, 0], states[:, 1], states[:, 2], grad, step_count)
+    lane_sums = jnp.sum(news[0] * weights, axis=1)
+    local_sums = (lane_sums[:, :HALF] + lane_sums[:, HALF:]).reshape(FEAT)
     spread = jnp.broadcast_to(local_sums, (Z * X, FEAT))
-    plane_sums = jnp.sum(lax.all_to_all(spread, ("z", "x"), 0, 0, tiled=True), axis=0)
-    checksum = plane_sums + swapped(plane_sums, "yh", YH, 1)
+    checksum = jnp.sum(lax.all_to_all(spread, ("z", "x"), 0, 0, tiled=True), axis=0)
+
+    def own(value):
+        mine = jnp.where(my_half == 0, value[:, :, :HALF], value[:, :, HALF:])
+        return jnp.concatenate([mine[0], mine[1]], axis=1)
+
+    new_master, new_first, new_second = (own(v) for v in news)
     params = new_master.astype(jnp.bfloat16)
     return (
         new_master.T[None],

time: 110 us -> 105 us (0.955)
  blocking collectives: 19 us -> 5.64 us
  starting transfers between devices: 35.4 us -> 46.7 us
  waiting for transfers between devices: 40.1 us -> 34.7 us
  local copies, waits for them, and re-layouts: 4.68 us -> 1.72 us
  Pallas kernels: 0 us -> 2.82 us
  other arithmetic: 6.13 us -> 8.93 us
    all_to_all x1 -> x0, blocking collectives: 13.9 us -> none  [shards(): lax.all_to_all(spread, ('z', 'x'), 0, 0, tiled=True)]
    all_to_all x1 -> x2, waiting for transfers between devices: 21.5 us -> 12.4 us  [the longest x1 6.64 us: reduced_grad(): lax.all_to_all(chip.reshape(Z * X, WIDTH, FEAT), ('z', 'x'), 0, 0, tiled=...]
    all_to_all x1 -> x2, starting transfers between devices: 7.65 us -> 13.7 us  [the longest x1 7.64 us: reduced_grad(): lax.all_to_all(chip.reshape(Z * X, WIDTH, FEAT), ('z', 'x'), 0, 0, tiled=...]
    ppermute x5, starting transfers between devices: 21 us -> 26.1 us  [swapped(): return lax.ppermute(value, axis, [(i, i ^ bit) for i in range(size)])]
    all_to_all x1, waiting for transfers between devices: 6.66 us -> 10.8 us  [reduced_grad(): lines = lax.all_to_all(spread, ('yh', 'yl'), 0, 0, tiled=True)]
    pallas_call x0 -> x2, Pallas kernels: none -> 2.82 us  [turned(): pl.pallas_call(turn_kernel, grid_spec=pltpu.PrefetchScalarGridSpec(num_sc...]
    unnamed x15 -> x12, local copies, waits for them, and re-layouts: 2.63 us -> 0.03 us
    add x1 -> x2, other arithmetic: 0.41 us -> 2.79 us  [the longest x1 2.71 us: chip_sum(): return (kept + given, beside)]
  transfers between devices with their start and end apart: 7 -> 8, of which waited for: 5 -> 6; matrix products, arithmetic and copies ran while one was open for 3% -> 8% of each run, Pallas kernels for 0% -> 1%
where the time goes in v2:
time: 105 us; the launch traced here: 104 us
  starting transfers between devices  46.7 us (44%)
  waiting for transfers between devices  34.7 us (33%)
  other arithmetic  8.93 us (9%)
  blocking collectives  5.64 us (5%)
  between operations  3.67 us (3%)
  Pallas kernels  2.82 us (3%)
  local copies, waits for them, and re-layouts  1.72 us (2%)
    ppermute x5, starting transfers between devices, swapped(): return lax.ppermute(value, axis, [(i, i ^ bit) for i in range(size)])  26.1 us
    ppermute x5, waiting for transfers between devices, swapped(): return lax.ppermute(value, axis, [(i, i ^ bit) for i in range(size)])  11.5 us
    all_to_all x1, waiting for transfers between devices, reduced_grad(): lines = lax.all_to_all(spread, ('yh', 'yl'), 0, 0, tiled=True)  10.8 us
    all_to_all x1, starting transfers between devices, reduced_grad(): lax.all_to_all(chip.reshape(Z * X, WIDTH, FEAT), ('z', 'x'), 0, 0, tiled=...  7.64 us
    all_to_all x1, starting transfers between devices, reduced_grad(): lines = lax.all_to_all(spread, ('yh', 'yl'), 0, 0, tiled=True)  6.82 us
    all_to_all x1, waiting for transfers between devices, reduced_grad(): lax.all_to_all(chip.reshape(Z * X, WIDTH, FEAT), ('z', 'x'), 0, 0, tiled=...  6.64 us
    all_to_all x1, starting transfers between devices, shards(): lax.all_to_all(spread, ('z', 'x'), 0, 0, tiled=True)  6.04 us
    all_to_all x1, waiting for transfers between devices, shards(): lax.all_to_all(spread, ('z', 'x'), 0, 0, tiled=True)  5.79 us
  transfers between devices with their start and end apart: 8, of which 6 were waited for; matrix products, arithmetic and copies ran while one was open for 8% of the time, Pallas kernels for 1%

profile of v2, /device:TPU:1, one launch (start us, length us, event | category | flops | bytes accessed | tf_op | source)
XLA Modules:
  0.0 104.2 jit_solution(8775292639787513792)
XLA Ops:
  0.6 1.4 %shard_map.120 = f32[3072,128]{1,0:T(8,128)S(1)} custom-call(s32[1]{0:T(128)} %bitcast.8.half_ref, bf16[128,6144]{1,0:T(8,128)(2,1)} %bitcast.88), custom_call_target="tpu_custom_call" | custom-call | bytes 2359296 | tf_op jit(solution)/shard_map/pallas_call | solution.py:48
  2.0 8.8 %collective-permute-start = (f32[3072,128]{1,0:T(8,128)S(1)}, f32[3072,128]{1,0:T(8,128)}, u32[]{:S(2)}, u32[]{:S(2)}) collective-permute-start(f32[3072,128]{1,0:T(8,128)S(1)} %shard_map.120), channel_id=1, source_target_pairs={{0,64},{64,0},{1,65},{65,1},{2,66},{66,2},{3,67},{67,3},{4,68},{68... | collective-permute-start | bytes 4718600 | tf_op jit(solution)/shard_map/ppermute | solution.py:22
  10.9 1.4 %shard_map.119 = f32[3072,128]{1,0:T(8,128)S(1)} custom-call(s32[1]{0:T(128)} %bitcast.half_ref, bf16[128,6144]{1,0:T(8,128)(2,1)} %bitcast.89), custom_call_target="tpu_custom_call" | custom-call | bytes 2359296 | tf_op jit(solution)/shard_map/pallas_call | solution.py:48
  12.4 1.9 %collective-permute-start.1 = (f32[288,128]{1,0:T(8,128)S(1)}, f32[288,128]{1,0:T(8,128)S(1)}, u32[]{:S(2)}, u32[]{:S(2)}) collective-permute-start(f32[288,128]{1,0:T(8,128)S(1)} %bitcast.90), channel_id=1, source_target_pairs={{0,64},{64,0},{1,65},{65,1},{2,66},{66,2},{3,67},{67,3},{4,68},{68... | collective-permute-start | bytes 442376 | tf_op jit(solution)/shard_map/ppermute | solution.py:22
  14.3 0.6 and_reduce_fusion
  15.0 2.7 %add.39 = f32[3072,128]{1,0:T(8,128)} add(f32[3072,128]{1,0:T(8,128)S(1)} %shard_map.119, f32[3072,128]{1,0:T(8,128)} %collective-permute-done) | non-fusion elementwise | flops 393216 | bytes 4718592 | tf_op jit(solution)/shard_map/add | solution.py:66
  17.7 7.6 %all-to-all-start = ((f32[32,96,128]{2,1,0:T(8,128)}), f32[32,96,128]{2,1,0:T(8,128)S(1)}, u32[]{:S(2)}, u32[]{:S(2)}) async-start(f32[32,96,128]{2,1,0:T(8,128)} %bitcast.9), calls=%async_computation | async-start | bytes 3145728 | tf_op jit(solution)/shard_map/all_to_all | solution.py:70
  25.3 0.6 fusion.6
  26.7 3.2 %collective-permute-start.2 = (f32[288,128]{1,0:T(8,128)S(1)}, f32[288,128]{1,0:T(8,128)S(1)}, u32[]{:S(2)}, u32[]{:S(2)}) collective-permute-start(f32[288,128]{1,0:T(8,128)S(1)} %broadcast_select_fusion.2), channel_id=1, source_target_pairs={{0,128},{128,0},{256,384},{384,256},{1,129},{129,1},{257,385},{385... | collective-permute-start | bytes 442376 | tf_op jit(solution)/shard_map/ppermute | solution.py:22
  30.5 2.6 %collective-permute-done.2 = f32[288,128]{1,0:T(8,128)S(1)} collective-permute-done((f32[288,128]{1,0:T(8,128)S(1)}, f32[288,128]{1,0:T(8,128)S(1)}, u32[]{:S(2)}, u32[]{:S(2)}) %collective-permute-start.2) | collective-permute-done | bytes 147488 | tf_op jit(solution)/shard_map/ppermute | solution.py:22
  33.2 4.2 %collective-permute-start.3 = (f32[288,128]{1,0:T(8,128)S(1)}, f32[288,128]{1,0:T(8,128)S(1)}, u32[]{:S(2)}, u32[]{:S(2)}) collective-permute-start(f32[288,128]{1,0:T(8,128)S(1)} %broadcast_select_fusion.3), channel_id=1, source_target_pairs={{0,256},{128,384},{256,0},{384,128},{1,257},{129,385},{257,1},{385... | collective-permute-start | bytes 442376 | tf_op jit(solution)/shard_map/ppermute | solution.py:22
  38.1 5.7 %collective-permute-done.3 = f32[288,128]{1,0:T(8,128)S(1)} collective-permute-done((f32[288,128]{1,0:T(8,128)S(1)}, f32[288,128]{1,0:T(8,128)S(1)}, u32[]{:S(2)}, u32[]{:S(2)}) %collective-permute-start.3) | collective-permute-done | bytes 147488 | tf_op jit(solution)/shard_map/ppermute | solution.py:22
  43.8 0.7 select_select_fusion
  44.5 8.0 %collective-permute-start.4 = (f32[296,128]{1,0:T(8,128)S(1)}, f32[296,128]{1,0:T(8,128)S(1)}, u32[]{:S(2)}, u32[]{:S(2)}) collective-permute-start(f32[296,128]{1,0:T(8,128)S(1)} %pad_maximum_fusion.1), channel_id=1, source_target_pairs={{0,32},{32,0},{1,33},{33,1},{2,34},{34,2},{3,35},{35,3},{4,36},{36... | collective-permute-start | bytes 454664 | tf_op jit(solution)/shard_map/ppermute | solution.py:22
  52.6 3.1 %collective-permute-done.4 = f32[296,128]{1,0:T(8,128)S(1)} collective-permute-done((f32[296,128]{1,0:T(8,128)S(1)}, f32[296,128]{1,0:T(8,128)S(1)}, u32[]{:S(2)}, u32[]{:S(2)}) %collective-permute-start.4) | collective-permute-done | bytes 151584 | tf_op jit(solution)/shard_map/ppermute | solution.py:22
  55.9 0.1 maximum_bitcast_fusion.1
  56.1 0.1 maximum_bitcast_fusion
  56.3 6.6 %all-to-all-done = f32[32,96,128]{2,1,0:T(8,128)S(1)} async-done(((f32[32,96,128]{2,1,0:T(8,128)}), f32[32,96,128]{2,1,0:T(8,128)S(1)}, u32[]{:S(2)}, u32[]{:S(2)}) %all-to-all-start) | async-done | bytes 1572896 | tf_op jit(solution)/shard_map/all_to_all | solution.py:70
  63.0 0.8 broadcast_in_dim.48
  63.8 6.8 %all-to-all-start.1 = ((f32[8,96,128]{2,1,0:T(8,128)}), f32[8,96,128]{2,1,0:T(8,128)S(1)}, u32[]{:S(2)}, u32[]{:S(2)}) async-start(f32[8,96,128]{2,1,0:T(8,128)} %broadcast_in_dim.48), calls=%async_computation.1 | async-start | bytes 786432 | tf_op jit(solution)/shard_map/all_to_all | solution.py:74
  71.4 10.8 %all-to-all-done.1 = f32[8,96,128]{2,1,0:T(8,128)S(1)} async-done(((f32[8,96,128]{2,1,0:T(8,128)}), f32[8,96,128]{2,1,0:T(8,128)S(1)}, u32[]{:S(2)}, u32[]{:S(2)}) %all-to-all-start.1) | async-done | bytes 393248 | tf_op jit(solution)/shard_map/all_to_all | solution.py:74
  82.2 5.6 %all-gather = f32[192,128]{1,0:T(8,128)S(1)} all-gather(f32[96,128]{1,0:T(8,128)S(1)} %reduce_sum.47), channel_id=2, replica_groups=mesh['yl'=4,'c'=2,'yh'=2,'z'=8,'x'=4] {'c'}, dimensions={0}, use_global_device_ids=true | all-gather | bytes 147456 | tf_op jit(solution)/shard_map/all_gather | solution.py:76
  87.8 0.1 multiply_reduce_fusion
  88.1 0.1 slice_select_fusion
  88.4 0.6 broadcast_in_dim.54
  89.0 6.0 %all-to-all-start.2 = ((f32[32,1,128]{2,1,0:T(1,128)}), f32[32,1,128]{2,1,0:T(1,128)S(1)}, u32[]{:S(2)}, u32[]{:S(2)}) async-start(f32[32,1,128]{2,1,0:T(1,128)} %broadcast_in_dim.54), calls=%async_computation.2 | async-start | bytes 32768 | tf_op jit(solution)/shard_map/all_to_all | solution.py:118
  95.0 0.7 fusion.5
  95.8 0.7 maximum_bitcast_fusion.2
  96.5 0.7 maximum_bitcast_fusion.3
  97.2 0.7 convert_bitcast_fusion
  97.8 5.8 %all-to-all-done.2 = f32[32,1,128]{2,1,0:T(1,128)S(1)} async-done(((f32[32,1,128]{2,1,0:T(1,128)}), f32[32,1,128]{2,1,0:T(1,128)S(1)}, u32[]{:S(2)}, u32[]{:S(2)}) %all-to-all-start.2) | async-done | bytes 16416 | tf_op jit(solution)/shard_map/all_to_all | solution.py:118
  103.6 0.5 reduce_sum.49
  (37 shorter events, 0.9 us)
Async XLA Ops:
  2.0 12.9 %collective-permute-start = (f32[3072,128]{1,0:T(8,128)S(1)}, f32[3072,128]{1,0:T(8,128)}, u32[]{:S(2)}, u32[]{:S(2)}) collective-permute-start(f32[3072,128]{1,0:T(8,128)S(1)} %shard_map.120), channel_id=1, source_target_pairs={{0,64},{64,0},{1,65},{65,1},{2,66},{66,2},{3,67},{67,3},{4,68},{68... | collective-permute-start | bytes 4718600 | tf_op jit(solution)/shard_map/ppermute | solution.py:22
  10.8 1.5 %copy-start = (f32[1,128,96]{1,2,0:T(8,128)S(1)}, f32[1,128,96]{1,2,0:T(8,128)}, u32[]{:S(2)}) copy-start(f32[1,128,96]{1,2,0:T(8,128)} %param.11) | copy-start | bytes 147460
  10.8 1.5 %copy-start.1 = (f32[1,128,96]{1,2,0:T(8,128)S(1)}, f32[1,128,96]{1,2,0:T(8,128)}, u32[]{:S(2)}) copy-start(f32[1,128,96]{1,2,0:T(8,128)} %param.10) | copy-start | bytes 147460
  10.9 1.5 %copy-start.2 = (f32[1,128,96]{1,2,0:T(8,128)S(1)}, f32[1,128,96]{1,2,0:T(8,128)}, u32[]{:S(2)}) copy-start(f32[1,128,96]{1,2,0:T(8,128)} %param.9) | copy-start | bytes 147460
  10.9 3.4 %copy-start.3 = (s32[8]{0:T(128)S(1)}, s32[8]{0:T(128)}, u32[]{:S(2)}) copy-start(s32[8]{0:T(128)} %param.13) | copy-start | bytes 100
  12.4 14.3 %collective-permute-start.1 = (f32[288,128]{1,0:T(8,128)S(1)}, f32[288,128]{1,0:T(8,128)S(1)}, u32[]{:S(2)}, u32[]{:S(2)}) collective-permute-start(f32[288,128]{1,0:T(8,128)S(1)} %bitcast.90), channel_id=1, source_target_pairs={{0,64},{64,0},{1,65},{65,1},{2,66},{66,2},{3,67},{67,3},{4,68},{68... | collective-permute-start | bytes 442376 | tf_op jit(solution)/shard_map/ppermute | solution.py:22
  17.7 7.7 %copy-start.4 = (s32[8]{0:T(128)S(1)}, s32[8]{0:T(128)}, u32[]{:S(2)}) copy-start(s32[8]{0:T(128)} %param.14) | copy-start | bytes 100
  17.7 20.4 %copy-start.5 = (f32[96]{0:T(128)S(1)}, f32[96]{0:T(128)}, u32[]{:S(2)}) copy-start(f32[96]{0:T(128)} %param.12) | copy-start | bytes 1156
  17.7 45.3 %all-to-all-start = ((f32[32,96,128]{2,1,0:T(8,128)}), f32[32,96,128]{2,1,0:T(8,128)S(1)}, u32[]{:S(2)}, u32[]{:S(2)}) async-start(f32[32,96,128]{2,1,0:T(8,128)} %bitcast.9), calls=%async_computation | async-start | bytes 3145728 | tf_op jit(solution)/shard_map/all_to_all | solution.py:70
  26.7 6.5 %collective-permute-start.2 = (f32[288,128]{1,0:T(8,128)S(1)}, f32[288,128]{1,0:T(8,128)S(1)}, u32[]{:S(2)}, u32[]{:S(2)}) collective-permute-start(f32[288,128]{1,0:T(8,128)S(1)} %broadcast_select_fusion.2), channel_id=1, source_target_pairs={{0,128},{128,0},{256,384},{384,256},{1,129},{129,1},{257,385},{385... | collective-permute-start | bytes 442376 | tf_op jit(solution)/shard_map/ppermute | solution.py:22
  33.2 10.6 %collective-permute-start.3 = (f32[288,128]{1,0:T(8,128)S(1)}, f32[288,128]{1,0:T(8,128)S(1)}, u32[]{:S(2)}, u32[]{:S(2)}) collective-permute-start(f32[288,128]{1,0:T(8,128)S(1)} %broadcast_select_fusion.3), channel_id=1, source_target_pairs={{0,256},{128,384},{256,0},{384,128},{1,257},{129,385},{257,1},{385... | collective-permute-start | bytes 442376 | tf_op jit(solution)/shard_map/ppermute | solution.py:22
  44.5 11.2 %collective-permute-start.4 = (f32[296,128]{1,0:T(8,128)S(1)}, f32[296,128]{1,0:T(8,128)S(1)}, u32[]{:S(2)}, u32[]{:S(2)}) collective-permute-start(f32[296,128]{1,0:T(8,128)S(1)} %pad_maximum_fusion.1), channel_id=1, source_target_pairs={{0,32},{32,0},{1,33},{33,1},{2,34},{34,2},{3,35},{35,3},{4,36},{36... | collective-permute-start | bytes 454664 | tf_op jit(solution)/shard_map/ppermute | solution.py:22
  63.8 18.3 %all-to-all-start.1 = ((f32[8,96,128]{2,1,0:T(8,128)}), f32[8,96,128]{2,1,0:T(8,128)S(1)}, u32[]{:S(2)}, u32[]{:S(2)}) async-start(f32[8,96,128]{2,1,0:T(8,128)} %broadcast_in_dim.48), calls=%async_computation.1 | async-start | bytes 786432 | tf_op jit(solution)/shard_map/all_to_all | solution.py:74
  89.0 14.6 %all-to-all-start.2 = ((f32[32,1,128]{2,1,0:T(1,128)}), f32[32,1,128]{2,1,0:T(1,128)S(1)}, u32[]{:S(2)}, u32[]{:S(2)}) async-start(f32[32,1,128]{2,1,0:T(1,128)} %broadcast_in_dim.54), calls=%async_computation.2 | async-start | bytes 32768 | tf_op jit(solution)/shard_map/all_to_all | solution.py:118

commit v3 on v2

v3 whole, which is shorter than its diff:
```python
import jax
import jax.numpy as jnp
from jax import lax
from jax.experimental import pallas as pl
from jax.experimental.pallas import tpu as pltpu
from jax.sharding import Mesh, PartitionSpec as P

beta_one = 0.9
beta_two = 0.95
learn_rate = 0.05
decay_rate = 0.1
epsilon = 1e-08

YL, C, YH, ZQ, ZB, X = 4, 2, 2, 4, 2, 4
Z = ZQ * ZB
REP = ("yl", "c")
FSDP = ("yh", "zq", "zb", "x")
WIDTH, HALF, FEAT = 96, 64, 128


def swapped(value, axis, size, bit):
    return lax.ppermute(value, axis, [(i, i ^ bit) for i in range(size)])


def corrections(step_count):
    steps_done = step_count[0].astype(jnp.float32)
    correct_one = 1.0 - jnp.power(jnp.float32(beta_one), steps_done)
    correct_two = 1.0 - jnp.power(jnp.float32(beta_two), steps_done)
    return correct_one, correct_two


def adamw_update(master, first, second, grad, correct_one, correct_two):
    new_first = beta_one * first + (1.0 - beta_one) * grad
    new_second = beta_two * second + (1.0 - beta_two) * (grad * grad)
    update = new_first / correct_one / (jnp.sqrt(new_second / correct_two) + epsilon)
    new_master = master - learn_rate * (update + decay_rate * master)
    return (new_master, new_first, new_second)


def give_kernel(half_ref, grad_ref, master_ref, first_ref, second_ref, turned_ref):
    turn_kernel(half_ref, grad_ref, turned_ref)
    start = Z * X * WIDTH
    for i, state_ref in enumerate((master_ref, first_ref, second_ref)):
        turned_ref[start + i * WIDTH : start + (i + 1) * WIDTH, :] = state_ref[...]


def turn_kernel(half_ref, grad_ref, turned_ref):
    columns = Z * X * WIDTH
    for z in range(Z):
        first = grad_ref[:, z * X * WIDTH : (z + 1) * X * WIDTH]
        second = grad_ref[:, columns + z * X * WIDTH : columns + (z + 1) * X * WIDTH]
        value = jnp.concatenate([first, second], axis=0).T.astype(jnp.float32)
        for x in range(X):
            place = ((z % ZB * X + x) * ZQ + z // ZB) * WIDTH
            turned_ref[place : place + WIDTH, :] = value[x * WIDTH : (x + 1) * WIDTH]


def turned(grad, half, *state):
    columns = Z * X * WIDTH
    rows = columns + len(state) * WIDTH
    return pl.pallas_call(
        give_kernel if state else turn_kernel,
        grid_spec=pltpu.PrefetchScalarGridSpec(
            num_scalar_prefetch=1,
            grid=(1,),
            in_specs=[pl.BlockSpec((HALF, YH * columns), lambda i, half_ref: (half_ref[0], 0))]
            + [pl.BlockSpec((WIDTH, FEAT), lambda i, half_ref: (0, 0))] * len(state),
            out_specs=pl.BlockSpec(memory_space=pltpu.VMEM),
        ),
        out_shape=pltpu.VMEM((rows, FEAT), jnp.float32),
        cost_estimate=pl.CostEstimate(flops=0, bytes_accessed=columns * FEAT * 6, transcendentals=0),
    )(half.reshape(1), grad, *state)


def chip_sum(grad_parts, state, *beside):
    core = lax.axis_index("c")
    grad = grad_parts[0, 0]
    given = swapped(turned(grad, 1 - core, *state), "c", C, 1)
    columns = Z * X * WIDTH
    kept, *beside = lax.optimization_barrier((turned(grad, core), *beside))
    return kept + given[:columns], given[columns:], *beside


def near_grad(chip):
    blocks = lax.all_to_all(
        chip.reshape(ZB * X, ZQ * WIDTH, FEAT), ("zb", "x"), 0, 0, tiled=True
    )
    return jnp.sum(blocks, axis=0).reshape(ZQ, WIDTH, FEAT)


def reduced_grad(near, beside):
    plane = jnp.sum(lax.all_to_all(near, "zq", 0, 0, tiled=True), axis=0)
    plane, beside = lax.optimization_barrier((plane, beside))
    spread = jnp.broadcast_to(plane, (YH * YL, WIDTH, FEAT))
    lines = lax.all_to_all(spread, ("yh", "yl"), 0, 0, tiled=True)
    line = jnp.sum(lines, axis=0)
    return lax.all_gather(line, "c", axis=0, tiled=False), beside


def way_to_donor(flagged, source):
    match = flagged % (YH * Z * X) == lax.axis_index(FSDP)
    replica = flagged // (YH * Z * X)
    way = jnp.sum(jnp.where(match, replica ^ source, 0))
    return way, jnp.any(match & (replica == lax.axis_index(REP)))


def healed_state(state, other, way, flagged_here):
    moved = jnp.where((way & 1) != 0, other, state)
    for bit, place in ((1, 2), (2, 4)):
        other = swapped(moved, "yl", YL, bit)
        moved = jnp.where((way & place) != 0, other, moved)
    return jnp.where(flagged_here, moved, state)


def shards(grad_parts, master, moment1, moment2, probe, flagged, source, step_count):
    my_half = lax.axis_index("yh")
    state = (master[0].T, moment1[0].T, moment2[0].T)
    chip, other, way, flagged_here, correct = chip_sum(
        grad_parts, state, *way_to_donor(flagged, source), corrections(step_count)
    )
    state = jnp.concatenate(state)
    healed = healed_state(state, other, way, flagged_here)
    near, healed = lax.optimization_barrier((near_grad(chip), healed))
    weights = jnp.pad(jnp.broadcast_to(probe, (8, WIDTH)), ((0, 0), (0, FEAT - WIDTH)))
    mine = jnp.concatenate([healed, weights])
    other = swapped(mine, "yh", YH, 1)
    low, high = jnp.where(my_half == 0, mine, other), jnp.where(my_half == 0, other, mine)
    packed = jnp.stack(
        [
            jnp.concatenate([low[: 3 * WIDTH, :HALF], high[: 3 * WIDTH, :HALF]], axis=1),
            jnp.concatenate([low[: 3 * WIDTH, HALF:], high[: 3 * WIDTH, HALF:]], axis=1),
        ]
    )
    first_lanes = lax.broadcasted_iota(jnp.int32, (WIDTH, FEAT), 1) < HALF
    weights = jnp.where(
        first_lanes, low[3 * WIDTH, :WIDTH, None], high[3 * WIDTH, :WIDTH, None]
    )
    grad, (packed, weights) = reduced_grad(near, (packed, weights))
    states = packed.reshape(C, 3, WIDTH, FEAT)
    news = adamw_update(states[:, 0], states[:, 1], states[:, 2], grad, *correct)
    lane_sums = jnp.sum(news[0] * weights, axis=1)
    local_sums = (lane_sums[:, :HALF] + lane_sums[:, HALF:]).reshape(FEAT)
    spread = jnp.broadcast_to(local_sums, (Z * X, FEAT))
    checksum = jnp.sum(lax.all_to_all(spread, ("zq", "zb", "x"), 0, 0, tiled=True), axis=0)

    def own(value):
        mine = jnp.where(my_half == 0, value[:, :, :HALF], value[:, :, HALF:])
        return jnp.concatenate([mine[0], mine[1]], axis=1)

    new_master, new_first, new_second = (own(v) for v in news)
    params = new_master.astype(jnp.bfloat16)
    return (
        new_master.T[None],
        new_first.T[None],
        new_second.T[None],
        params.T[None],
        checksum.reshape(1, -1),
    )


def solution(mesh):
    named = Mesh(mesh.devices.reshape(YL, C, YH, ZQ, ZB, X), REP + FSDP)
    state = P(REP, None, FSDP)
    placed = (P(REP, FSDP, None, None), state, state, state, P(FSDP), P(), P(), P())
    return jax.shard_map(
        shards,
        mesh=named,
        in_specs=placed,
        out_specs=(state, state, state, state, P(REP, None)),
        check_vma=False,
    )
```

time: 105 us -> 99.7 us (0.950)
  blocking collectives: 5.64 us -> 19.6 us
  starting transfers between devices: 46.7 us -> 35.1 us
  waiting for transfers between devices: 34.7 us -> 26.4 us
  other arithmetic: 8.93 us -> 10.5 us
    all_to_all x0 -> x1, blocking collectives: none -> 13 us  [reduced_grad(): lines = lax.all_to_all(spread, ('yh', 'yl'), 0, 0, tiled=True)]
    all_to_all x3, waiting for transfers between devices: 23.2 us -> 11 us  [the longest x1 5.63 us: shards(): lax.all_to_all(spread, ('zq', 'zb', 'x'), 0, 0, tiled=True)]
    ppermute x5 -> x4, starting transfers between devices: 26.1 us -> 16.5 us  [swapped(): return lax.ppermute(value, axis, [(i, i ^ bit) for i in range(size)])]
    ppermute x5 -> x4, waiting for transfers between devices: 11.5 us -> 15.4 us  [swapped(): return lax.ppermute(value, axis, [(i, i ^ bit) for i in range(size)])]
    all_to_all x3, starting transfers between devices: 20.5 us -> 18.6 us  [the longest x1 9.13 us: reduced_grad(): plane = jnp.sum(lax.all_to_all(near, 'zq', 0, 0, tiled=True), axis=0)]
  transfers between devices with their start and end apart: 8 -> 7, of which waited for: 6 -> 5; matrix products, arithmetic and copies ran while one was open for 8% -> 6% of each run, Pallas kernels for 1% -> 1%
where the time goes in v3:
time: 99.7 us; the launch traced here: 99 us
  starting transfers between devices  35.1 us (35%)
  waiting for transfers between devices  26.4 us (26%)
  blocking collectives  19.6 us (20%)
  other arithmetic  10.5 us (11%)
  between operations  3.61 us (4%)
  Pallas kernels  2.83 us (3%)
    ppermute x4, starting transfers between devices, swapped(): return lax.ppermute(value, axis, [(i, i ^ bit) for i in range(size)])  16.5 us
    ppermute x4, waiting for transfers between devices, swapped(): return lax.ppermute(value, axis, [(i, i ^ bit) for i in range(size)])  15.4 us
    all_to_all x1, blocking collectives, reduced_grad(): lines = lax.all_to_all(spread, ('yh', 'yl'), 0, 0, tiled=True)  13 us
    all_to_all x1, starting transfers between devices, reduced_grad(): plane = jnp.sum(lax.all_to_all(near, 'zq', 0, 0, tiled=True), axis=0)  9.13 us
    all_gather x1, blocking collectives, reduced_grad(): return (lax.all_gather(line, 'c', axis=0, tiled=False), beside)  6.6 us
    all_to_all x1, starting transfers between devices, shards(): lax.all_to_all(spread, ('zq', 'zb', 'x'), 0, 0, tiled=True)  5.76 us
    all_to_all x1, waiting for transfers between devices, shards(): lax.all_to_all(spread, ('zq', 'zb', 'x'), 0, 0, tiled=True)  5.63 us
    all_to_all x1, waiting for transfers between devices, reduced_grad(): plane = jnp.sum(lax.all_to_all(near, 'zq', 0, 0, tiled=True), axis=0)  5.37 us
  transfers between devices with their start and end apart: 7, of which 5 were waited for; matrix products, arithmetic and copies ran while one was open for 6% of the time, Pallas kernels for 1%

profile of v3, /device:TPU:1, one launch (start us, length us, event | category | flops | bytes accessed | tf_op | source)
XLA Modules:
  0.0 99.0 jit_solution(7526039407283209834)
XLA Ops:
  0.6 1.4 %shard_map.120 = f32[3360,128]{1,0:T(8,128)S(1)} custom-call(s32[1]{0:T(128)} %bitcast.4.half_ref, bf16[128,6144]{1,0:T(8,128)(2,1)} %bitcast.92, f32[96,128]{1,0:T(8,128)} %bitcast.95, f32[96,128]{1,0:T(8,128)} %bitcast.98, f32[96,128]{1,0:T(8,128)} %bitcast.101), custom_call_target="tpu_custom_call" | custom-call | bytes 2359296 | tf_op jit(solution)/shard_map/pallas_call | solution.py:61
  2.1 8.8 %collective-permute-start = (f32[3360,128]{1,0:T(8,128)S(1)}, f32[3360,128]{1,0:T(8,128)}, u32[]{:S(2)}, u32[]{:S(2)}) collective-permute-start(f32[3360,128]{1,0:T(8,128)S(1)} %shard_map.120), channel_id=1, source_target_pairs={{0,64},{64,0},{1,65},{65,1},{2,66},{66,2},{3,67},{67,3},{4,68},{68... | collective-permute-start | bytes 5160968 | tf_op jit(solution)/shard_map/ppermute | solution.py:22
  10.9 1.4 %shard_map.119 = f32[3072,128]{1,0:T(8,128)S(1)} custom-call(s32[1]{0:T(128)} %bitcast.half_ref, bf16[128,6144]{1,0:T(8,128)(2,1)} %bitcast.93), custom_call_target="tpu_custom_call" | custom-call | bytes 2359296 | tf_op jit(solution)/shard_map/pallas_call | solution.py:61
  13.1 0.6 and_reduce_fusion
  13.7 0.6 fusion.7
  14.3 2.7 %slice_add_fusion = f32[3072,128]{1,0:T(8,128)} fusion(f32[3072,128]{1,0:T(8,128)S(1)} %shard_map.119, f32[3360,128]{1,0:T(8,128)} %collective-permute-done), kind=kLoop, calls=%fused_computation | loop fusion | flops 393216 | bytes 4718592 | tf_op jit(solution)/shard_map/add | solution.py:81
  17.1 3.7 %all-to-all-start = ((f32[8,384,128]{2,1,0:T(8,128)}), f32[8,384,128]{2,1,0:T(8,128)S(1)}, u32[]{:S(2)}, u32[]{:S(2)}) async-start(f32[8,384,128]{2,1,0:T(8,128)} %bitcast.11), calls=%async_computation | async-start | bytes 3145728 | tf_op jit(solution)/shard_map/all_to_all | solution.py:85
  21.5 0.9 slice_select_fusion
  22.4 1.9 %collective-permute-start.1 = (f32[288,128]{1,0:T(8,128)S(1)}, f32[288,128]{1,0:T(8,128)S(1)}, u32[]{:S(2)}, u32[]{:S(2)}) collective-permute-start(f32[288,128]{1,0:T(8,128)S(1)} %slice_select_fusion), channel_id=1, source_target_pairs={{0,128},{128,0},{256,384},{384,256},{1,129},{129,1},{257,385},{385... | collective-permute-start | bytes 442376 | tf_op jit(solution)/shard_map/ppermute | solution.py:22
  25.0 4.5 %collective-permute-done.1 = f32[288,128]{1,0:T(8,128)S(1)} collective-permute-done((f32[288,128]{1,0:T(8,128)S(1)}, f32[288,128]{1,0:T(8,128)S(1)}, u32[]{:S(2)}, u32[]{:S(2)}) %collective-permute-start.1) | collective-permute-done | bytes 147488 | tf_op jit(solution)/shard_map/ppermute | solution.py:22
  29.5 1.9 %collective-permute-start.2 = (f32[288,128]{1,0:T(8,128)S(1)}, f32[288,128]{1,0:T(8,128)S(1)}, u32[]{:S(2)}, u32[]{:S(2)}) collective-permute-start(f32[288,128]{1,0:T(8,128)S(1)} %broadcast_select_fusion.2), channel_id=1, source_target_pairs={{0,256},{128,384},{256,0},{384,128},{1,257},{129,385},{257,1},{385... | collective-permute-start | bytes 442376 | tf_op jit(solution)/shard_map/ppermute | solution.py:22
  32.1 9.1 %collective-permute-done.2 = f32[288,128]{1,0:T(8,128)S(1)} collective-permute-done((f32[288,128]{1,0:T(8,128)S(1)}, f32[288,128]{1,0:T(8,128)S(1)}, u32[]{:S(2)}, u32[]{:S(2)}) %collective-permute-start.2) | collective-permute-done | bytes 147488 | tf_op jit(solution)/shard_map/ppermute | solution.py:22
  41.2 0.7 select_select_fusion
  41.9 0.8 reduce_sum.55
  42.6 3.9 %collective-permute-start.3 = (f32[296,128]{1,0:T(8,128)S(1)}, f32[296,128]{1,0:T(8,128)S(1)}, u32[]{:S(2)}, u32[]{:S(2)}) collective-permute-start(f32[296,128]{1,0:T(8,128)S(1)} %pad_maximum_fusion.1), channel_id=1, source_target_pairs={{0,32},{32,0},{1,33},{33,1},{2,34},{34,2},{3,35},{35,3},{4,36},{36... | collective-permute-start | bytes 454664 | tf_op jit(solution)/shard_map/ppermute | solution.py:22
  46.5 9.1 %all-to-all-start.1 = ((f32[4,96,128]{2,1,0:T(8,128)}), f32[4,96,128]{2,1,0:T(8,128)S(1)}, u32[]{:S(2)}, u32[]{:S(2)}) async-start(f32[4,96,128]{2,1,0:T(8,128)} %bitcast.12), calls=%async_computation.1 | async-start | bytes 393216 | tf_op jit(solution)/shard_map/all_to_all | solution.py:92
  55.7 1.8 %collective-permute-done.3 = f32[296,128]{1,0:T(8,128)S(1)} collective-permute-done((f32[296,128]{1,0:T(8,128)S(1)}, f32[296,128]{1,0:T(8,128)S(1)}, u32[]{:S(2)}, u32[]{:S(2)}) %collective-permute-start.3) | collective-permute-done | bytes 151584 | tf_op jit(solution)/shard_map/ppermute | solution.py:22
  57.7 0.1 maximum_bitcast_fusion.1
  57.9 0.1 maximum_bitcast_fusion
  58.1 5.4 %all-to-all-done.1 = f32[4,96,128]{2,1,0:T(8,128)S(1)} async-done(((f32[4,96,128]{2,1,0:T(8,128)}), f32[4,96,128]{2,1,0:T(8,128)S(1)}, u32[]{:S(2)}, u32[]{:S(2)}) %all-to-all-start.1) | async-done | bytes 196640 | tf_op jit(solution)/shard_map/all_to_all | solution.py:92
  63.5 13.0 %all_to_all.21 = f32[8,96,128]{2,1,0:T(8,128)S(1)} all-to-all(f32[8,96,128]{2,1,0:T(8,128)S(1)} %broadcast_in_dim.48), channel_id=1, replica_groups=mesh['yl'=4,'c'=2,'yh'=2,'zq'=4,'zb'=2,'x'=4] {'yh','yl'}, dimensions={0} | all-to-all | bytes 786432 | tf_op jit(solution)/shard_map/all_to_all | solution.py:95
  76.5 6.6 %all-gather = f32[192,128]{1,0:T(8,128)S(1)} all-gather(f32[96,128]{1,0:T(8,128)S(1)} %reduce_sum.57), channel_id=2, replica_groups=mesh['yl'=4,'c'=2,'yh'=2,'zq'=4,'zb'=2,'x'=4] {'c'}, dimensions={0}, use_global_device_ids=true | all-gather | bytes 147456 | tf_op jit(solution)/shard_map/all_gather | solution.py:97
  83.2 0.1 multiply_reduce_fusion
  83.4 0.1 slice_select_fusion.1
  83.7 0.6 broadcast_in_dim.54
  84.3 5.8 %all-to-all-start.3 = ((f32[32,1,128]{2,1,0:T(1,128)}), f32[32,1,128]{2,1,0:T(1,128)S(1)}, u32[]{:S(2)}, u32[]{:S(2)}) async-start(f32[32,1,128]{2,1,0:T(1,128)} %broadcast_in_dim.54), calls=%async_computation.3 | async-start | bytes 32768 | tf_op jit(solution)/shard_map/all_to_all | solution.py:144
  90.1 0.7 fusion.6
  90.8 0.7 maximum_bitcast_fusion.2
  91.5 0.7 maximum_bitcast_fusion.3
  92.2 0.7 convert_bitcast_fusion
  92.9 5.6 %all-to-all-done.3 = f32[32,1,128]{2,1,0:T(1,128)S(1)} async-done(((f32[32,1,128]{2,1,0:T(1,128)}), f32[32,1,128]{2,1,0:T(1,128)S(1)}, u32[]{:S(2)}, u32[]{:S(2)}) %all-to-all-start.3) | async-done | bytes 16416 | tf_op jit(solution)/shard_map/all_to_all | solution.py:144
  98.5 0.5 reduce_sum.59
  (36 shorter events, 0.8 us)
Async XLA Ops:
  2.1 12.3 %collective-permute-start = (f32[3360,128]{1,0:T(8,128)S(1)}, f32[3360,128]{1,0:T(8,128)}, u32[]{:S(2)}, u32[]{:S(2)}) collective-permute-start(f32[3360,128]{1,0:T(8,128)S(1)} %shard_map.120), channel_id=1, source_target_pairs={{0,64},{64,0},{1,65},{65,1},{2,66},{66,2},{3,67},{67,3},{4,68},{68... | collective-permute-start | bytes 5160968 | tf_op jit(solution)/shard_map/ppermute | solution.py:22
  10.9 2.2 %copy-start.3 = (s32[8]{0:T(128)S(1)}, s32[8]{0:T(128)}, u32[]{:S(2)}) copy-start(s32[8]{0:T(128)} %param.13) | copy-start | bytes 100
  10.9 2.8 %copy-start.4 = (s32[8]{0:T(128)S(1)}, s32[8]{0:T(128)}, u32[]{:S(2)}) copy-start(s32[8]{0:T(128)} %param.14) | copy-start | bytes 100
  17.0 4.4 %copy-start = (f32[1,128,96]{1,2,0:T(8,128)S(1)}, f32[1,128,96]{1,2,0:T(8,128)}, u32[]{:S(2)}) copy-start(f32[1,128,96]{1,2,0:T(8,128)} %param.9) | copy-start | bytes 147460
  17.1 4.4 %copy-start.1 = (f32[1,128,96]{1,2,0:T(8,128)S(1)}, f32[1,128,96]{1,2,0:T(8,128)}, u32[]{:S(2)}) copy-start(f32[1,128,96]{1,2,0:T(8,128)} %param.10) | copy-start | bytes 147460
  17.1 4.4 %copy-start.2 = (f32[1,128,96]{1,2,0:T(8,128)S(1)}, f32[1,128,96]{1,2,0:T(8,128)}, u32[]{:S(2)}) copy-start(f32[1,128,96]{1,2,0:T(8,128)} %param.11) | copy-start | bytes 147460
  17.1 15.0 %copy-start.5 = (f32[96]{0:T(128)S(1)}, f32[96]{0:T(128)}, u32[]{:S(2)}) copy-start(f32[96]{0:T(128)} %param.12) | copy-start | bytes 1156
  17.1 24.8 %all-to-all-start = ((f32[8,384,128]{2,1,0:T(8,128)}), f32[8,384,128]{2,1,0:T(8,128)S(1)}, u32[]{:S(2)}, u32[]{:S(2)}) async-start(f32[8,384,128]{2,1,0:T(8,128)} %bitcast.11), calls=%async_computation | async-start | bytes 3145728 | tf_op jit(solution)/shard_map/all_to_all | solution.py:85
  22.4 7.1 %collective-permute-start.1 = (f32[288,128]{1,0:T(8,128)S(1)}, f32[288,128]{1,0:T(8,128)S(1)}, u32[]{:S(2)}, u32[]{:S(2)}) collective-permute-start(f32[288,128]{1,0:T(8,128)S(1)} %slice_select_fusion), channel_id=1, source_target_pairs={{0,128},{128,0},{256,384},{384,256},{1,129},{129,1},{257,385},{385... | collective-permute-start | bytes 442376 | tf_op jit(solution)/shard_map/ppermute | solution.py:22
  29.5 11.7 %collective-permute-start.2 = (f32[288,128]{1,0:T(8,128)S(1)}, f32[288,128]{1,0:T(8,128)S(1)}, u32[]{:S(2)}, u32[]{:S(2)}) collective-permute-start(f32[288,128]{1,0:T(8,128)S(1)} %broadcast_select_fusion.2), channel_id=1, source_target_pairs={{0,256},{128,384},{256,0},{384,128},{1,257},{129,385},{257,1},{385... | collective-permute-start | bytes 442376 | tf_op jit(solution)/shard_map/ppermute | solution.py:22
  42.6 14.8 %collective-permute-start.3 = (f32[296,128]{1,0:T(8,128)S(1)}, f32[296,128]{1,0:T(8,128)S(1)}, u32[]{:S(2)}, u32[]{:S(2)}) collective-permute-start(f32[296,128]{1,0:T(8,128)S(1)} %pad_maximum_fusion.1), channel_id=1, source_target_pairs={{0,32},{32,0},{1,33},{33,1},{2,34},{34,2},{3,35},{35,3},{4,36},{36... | collective-permute-start | bytes 454664 | tf_op jit(solution)/shard_map/ppermute | solution.py:22
  46.5 16.9 %all-to-all-start.1 = ((f32[4,96,128]{2,1,0:T(8,128)}), f32[4,96,128]{2,1,0:T(8,128)S(1)}, u32[]{:S(2)}, u32[]{:S(2)}) async-start(f32[4,96,128]{2,1,0:T(8,128)} %bitcast.12), calls=%async_computation.1 | async-start | bytes 393216 | tf_op jit(solution)/shard_map/all_to_all | solution.py:92
  84.3 14.2 %all-to-all-start.3 = ((f32[32,1,128]{2,1,0:T(1,128)}), f32[32,1,128]{2,1,0:T(1,128)S(1)}, u32[]{:S(2)}, u32[]{:S(2)}) async-start(f32[32,1,128]{2,1,0:T(1,128)} %broadcast_in_dim.54), calls=%async_computation.3 | async-start | bytes 32768 | tf_op jit(solution)/shard_map/all_to_all | solution.py:144

commit v4 on v3

v4 whole, which is shorter than its diff:
```python
import itertools

import jax
import jax.numpy as jnp
from jax import lax
from jax.experimental import pallas as pl
from jax.experimental.pallas import tpu as pltpu
from jax.sharding import Mesh, PartitionSpec as P

beta_one = 0.9
beta_two = 0.95
learn_rate = 0.05
decay_rate = 0.1
epsilon = 1e-08

YL, C, YH, Z, X = 4, 2, 2, 8, 4
REP = ("yl", "c")
FSDP = ("yh", "z", "x")
WIDTH, HALF, FEAT, ROWS = 96, 64, 128, 48


def swapped(value, axis, size, bit):
    return lax.ppermute(value, axis, [(i, i ^ bit) for i in range(size)])


def corrections(step_count):
    steps_done = step_count[0].astype(jnp.float32)
    correct_one = 1.0 - jnp.power(jnp.float32(beta_one), steps_done)
    correct_two = 1.0 - jnp.power(jnp.float32(beta_two), steps_done)
    return correct_one, correct_two


def adamw_update(master, first, second, grad, correct_one, correct_two):
    new_first = beta_one * first + (1.0 - beta_one) * grad
    new_second = beta_two * second + (1.0 - beta_two) * (grad * grad)
    update = new_first / correct_one / (jnp.sqrt(new_second / correct_two) + epsilon)
    new_master = master - learn_rate * (update + decay_rate * master)
    return (new_master, new_first, new_second)


def give_kernel(half_ref, grad_ref, master_ref, first_ref, second_ref, turned_ref):
    turn_kernel(half_ref, grad_ref, turned_ref)
    start = Z * X * WIDTH
    for i, state_ref in enumerate((master_ref, first_ref, second_ref)):
        turned_ref[start + i * WIDTH : start + (i + 1) * WIDTH, :] = state_ref[...]


def near_place(core, z, x):
    z, x = (z - core) % Z, (x - core) % X
    return z % 2 * 2 + x % 2, z // 2 * 2 + x // 2


def turn_kernel(half_ref, grad_ref, turned_ref):
    columns = Z * X * WIDTH
    wide = X * WIDTH
    for half in range(C):

        @pl.when(half_ref[0] == half)
        def _():
            for z in range(Z):
                first = grad_ref[:, z * wide : (z + 1) * wide]
                second = grad_ref[:, columns + z * wide : columns + (z + 1) * wide]
                value = jnp.concatenate([first, second], axis=0).T.astype(jnp.float32)
                for x in range(X):
                    near, far = near_place(half, z, x)
                    row = (near * 8 + far) * WIDTH
                    turned_ref[row : row + WIDTH, :] = value[x * WIDTH : (x + 1) * WIDTH]


def turned(grad, half, *state):
    columns = Z * X * WIDTH
    rows = columns + len(state) * WIDTH
    return pl.pallas_call(
        give_kernel if state else turn_kernel,
        grid_spec=pltpu.PrefetchScalarGridSpec(
            num_scalar_prefetch=1,
            grid=(1,),
            in_specs=[pl.BlockSpec((HALF, YH * columns), lambda i, half_ref: (half_ref[0], 0))]
            + [pl.BlockSpec((WIDTH, FEAT), lambda i, half_ref: (0, 0))] * len(state),
            out_specs=pl.BlockSpec(memory_space=pltpu.VMEM),
        ),
        out_shape=pltpu.VMEM((rows, FEAT), jnp.float32),
        cost_estimate=pl.CostEstimate(flops=0, bytes_accessed=columns * FEAT * 6, transcendentals=0),
    )(half.reshape(1), grad, *state)


def chip_sum(grad_parts, state, *beside):
    core = lax.axis_index("c")
    grad = grad_parts[0, 0]
    given = swapped(turned(grad, 1 - core, *state), "c", C, 1)
    columns = Z * X * WIDTH
    kept, *beside = lax.optimization_barrier((turned(grad, core), *beside))
    return kept + given[:columns], given[columns:], *beside


def groups(over_near):
    found = {}
    for yl, c, yh, z, x in itertools.product(*map(range, (YL, C, YH, Z, X))):
        near, far = near_place(c, z, x)
        rank, rest = (near, far) if over_near else (far, near)
        device = (((yl * C + c) * YH + yh) * Z + z) * X + x
        found.setdefault((yl, c, yh, rest), {})[rank] = device
    return [[members[rank] for rank in sorted(members)] for members in found.values()]


def exchanged(blocks, over_near):
    every = ("yl", "c", "yh", "z", "x")
    return lax.all_to_all(blocks, every, 0, 0, tiled=True, axis_index_groups=groups(over_near))


def two_up(value, lanes):
    part = value[..., lanes * HALF : (lanes + 1) * HALF]
    return jnp.concatenate([part[..., :ROWS, :], part[..., ROWS:, :]], axis=-1)


def line_grad(plane):
    spread = jnp.stack([two_up(plane, half) for half in range(YH) for _ in range(YL)])
    lines = lax.all_to_all(spread, ("yh", "yl"), 0, 0, tiled=True)
    return lax.all_gather(jnp.sum(lines, axis=0), "c", axis=0, tiled=False)


def stage(moved, way, axis, size, bit, place):
    return jnp.where((way & place) != 0, swapped(moved, axis, size, bit), moved)


def way_to_donor(flagged, source):
    match = flagged % (YH * Z * X) == lax.axis_index(FSDP)
    replica = flagged // (YH * Z * X)
    way = jnp.sum(jnp.where(match, replica ^ source, 0))
    return way, jnp.any(match & (replica == lax.axis_index(REP)))


def shards(grad_parts, master, moment1, moment2, probe, flagged, source, step_count):
    state = (master[0].T, moment1[0].T, moment2[0].T)
    chip, other, way, flagged_here, correct = chip_sum(
        grad_parts, state, *way_to_donor(flagged, source), corrections(step_count)
    )
    state = jnp.concatenate(state)
    moved = jnp.where((way & 1) != 0, other, state)
    blocks = exchanged(chip.reshape(4, 8 * WIDTH, FEAT), True)
    near = jnp.sum(blocks, axis=0).reshape(8, WIDTH, FEAT)
    near, moved = lax.optimization_barrier((near, stage(moved, way, "yl", YL, 2, 4)))
    plane = jnp.sum(exchanged(near, False), axis=0)
    plane, moved = lax.optimization_barrier((plane, stage(moved, way, "yl", YL, 1, 2)))
    healed = jnp.where(flagged_here, moved, state).reshape(3, WIDTH, FEAT)
    packed = jnp.stack([two_up(healed, half) for half in range(C)])
    upper = lax.broadcasted_iota(jnp.int32, (ROWS, FEAT), 1) < HALF
    weights = jnp.where(upper, probe[:ROWS, None], probe[ROWS:, None])
    plane, packed, weights = lax.optimization_barrier((plane, packed, weights))
    grad = line_grad(plane)
    news = adamw_update(packed[:, 0], packed[:, 1], packed[:, 2], grad, *correct)
    lane_sums = jnp.sum(news[0] * weights, axis=1)
    local_sums = (lane_sums[:, :HALF] + lane_sums[:, HALF:]).reshape(FEAT)
    spread = jnp.broadcast_to(local_sums, (YH * Z * X, FEAT))
    checksum = jnp.sum(lax.all_to_all(spread, FSDP, 0, 0, tiled=True), axis=0)

    def own(value):
        upper = jnp.concatenate([value[0, :, :HALF], value[1, :, :HALF]], axis=1)
        lower = jnp.concatenate([value[0, :, HALF:], value[1, :, HALF:]], axis=1)
        return jnp.concatenate([upper, lower])

    new_master, new_first, new_second = (own(v) for v in news)
    params = new_master.astype(jnp.bfloat16)
    return (
        new_master.T[None],
        new_first.T[None],
        new_second.T[None],
        params.T[None],
        checksum.reshape(1, -1),
    )


def solution(mesh):
    named = Mesh(mesh.devices.reshape(YL, C, YH, Z, X), REP + FSDP)
    state = P(REP, None, FSDP)
    placed = (P(REP, FSDP, None, None), state, state, state, P(FSDP), P(), P(), P())
    return jax.shard_map(
        shards,
        mesh=named,
        in_specs=placed,
        out_specs=(state, state, state, state, P(REP, None)),
        check_vma=False,
    )
```

time: 99.7 us -> 98.9 us (level)
  waiting for transfers between devices: 26.4 us -> 20.1 us
  starting transfers between devices: 35.1 us -> 39.1 us
  blocking collectives: 19.6 us -> 21.1 us
    ppermute x4 -> x3, waiting for transfers between devices: 15.4 us -> 7.27 us  [swapped(): return lax.ppermute(value, axis, [(i, i ^ bit) for i in range(size)])]
    all_to_all x3, starting transfers between devices: 18.6 us -> 23.4 us  [the longest x2 16.8 us: exchanged(): lax.all_to_all(blocks, every, 0, 0, tiled=True, axis_index_groups=groups(...]
    all_to_all x1, blocking collectives: 13 us -> 15.8 us  [line_grad(): lines = lax.all_to_all(spread, ('yh', 'yl'), 0, 0, tiled=True)]
    all_to_all x3, waiting for transfers between devices: 11 us -> 12.8 us  [the longest x1 10.5 us: shards(): checksum = jnp.sum(lax.all_to_all(spread, FSDP, 0, 0, tiled=True), axis=0)]
    all_gather x1, blocking collectives: 6.6 us -> 5.24 us  [line_grad(): return lax.all_gather(jnp.sum(lines, axis=0), 'c', axis=0, tiled=False)]
    ppermute x4 -> x3, starting transfers between devices: 16.5 us -> 15.7 us  [swapped(): return lax.ppermute(value, axis, [(i, i ^ bit) for i in range(size)])]
  transfers between devices with their start and end apart: 7 -> 6, of which waited for: 5 -> 4; matrix products, arithmetic and copies ran while one was open for 6% -> 5% of each run, Pallas kernels for 1% -> 1%
where the time goes in v4:
time: 98.9 us; the launch traced here: 98.2 us
  starting transfers between devices  39.1 us (40%)
  blocking collectives  21.1 us (21%)
  waiting for transfers between devices  20.1 us (20%)
  other arithmetic  10.4 us (11%)
  between operations  3.54 us (4%)
  Pallas kernels  2.87 us (3%)
  local copies, waits for them, and re-layouts  1.27 us (1%)
    all_to_all x2, starting transfers between devices, exchanged(): lax.all_to_all(blocks, every, 0, 0, tiled=True, axis_index_groups=groups(...  16.8 us
    all_to_all x1, blocking collectives, line_grad(): lines = lax.all_to_all(spread, ('yh', 'yl'), 0, 0, tiled=True)  15.8 us
    ppermute x3, starting transfers between devices, swapped(): return lax.ppermute(value, axis, [(i, i ^ bit) for i in range(size)])  15.7 us
    all_to_all x1, waiting for transfers between devices, shards(): checksum = jnp.sum(lax.all_to_all(spread, FSDP, 0, 0, tiled=True), axis=0)  10.5 us
    ppermute x3, waiting for transfers between devices, swapped(): return lax.ppermute(value, axis, [(i, i ^ bit) for i in range(size)])  7.27 us
    all_to_all x1, starting transfers between devices, shards(): checksum = jnp.sum(lax.all_to_all(spread, FSDP, 0, 0, tiled=True), axis=0)  6.56 us
    all_gather x1, blocking collectives, line_grad(): return lax.all_gather(jnp.sum(lines, axis=0), 'c', axis=0, tiled=False)  5.24 us
    pallas_call x2, Pallas kernels, turned(): pl.pallas_call(give_kernel if state else turn_kernel, grid_spec=pltpu.Pre...  2.87 us
  transfers between devices with their start and end apart: 6, of which 4 were waited for; matrix products, arithmetic and copies ran while one was open for 5% of the time, Pallas kernels for 1%

profile of v4, /device:TPU:1, one launch (start us, length us, event | category | flops | bytes accessed | tf_op | source)
XLA Modules:
  0.0 98.2 jit_solution(17122680427138647259)
XLA Ops:
  0.6 1.5 %shard_map.120 = f32[3360,128]{1,0:T(8,128)S(1)} custom-call(s32[1]{0:T(128)} %bitcast.4.half_ref, bf16[128,6144]{1,0:T(8,128)(2,1)} %bitcast.89, f32[96,128]{1,0:T(8,128)} %bitcast.92, f32[96,128]{1,0:T(8,128)} %bitcast.95, f32[96,128]{1,0:T(8,128)} %bitcast.98), custom_call_target="tpu_custom_call" | custom-call | bytes 2359296 | tf_op jit(solution)/shard_map/pallas_call | solution.py:73
  2.1 8.8 %collective-permute-start = (f32[3360,128]{1,0:T(8,128)S(1)}, f32[3360,128]{1,0:T(8,128)}, u32[]{:S(2)}, u32[]{:S(2)}) collective-permute-start(f32[3360,128]{1,0:T(8,128)S(1)} %shard_map.120), channel_id=1, source_target_pairs={{0,64},{64,0},{1,65},{65,1},{2,66},{66,2},{3,67},{67,3},{4,68},{68... | collective-permute-start | bytes 5160968 | tf_op jit(solution)/shard_map/ppermute | solution.py:23
  10.9 1.4 %shard_map.119 = f32[3072,128]{1,0:T(8,128)S(1)} custom-call(s32[1]{0:T(128)} %bitcast.half_ref, bf16[128,6144]{1,0:T(8,128)(2,1)} %bitcast.90), custom_call_target="tpu_custom_call" | custom-call | bytes 2359296 | tf_op jit(solution)/shard_map/pallas_call | solution.py:73
  13.1 0.6 and_reduce_fusion
  13.7 0.6 fusion.4
  14.4 2.7 %slice_add_fusion = f32[3072,128]{1,0:T(8,128)} fusion(f32[3072,128]{1,0:T(8,128)S(1)} %shard_map.119, f32[3360,128]{1,0:T(8,128)} %collective-permute-done), kind=kLoop, calls=%fused_computation | loop fusion | flops 393216 | bytes 4718592 | tf_op jit(solution)/shard_map/add | solution.py:93
  17.1 9.2 %all-to-all-start = ((f32[4,768,128]{2,1,0:T(8,128)}), f32[4,768,128]{2,1,0:T(8,128)S(1)}, u32[]{:S(2)}, u32[]{:S(2)}) async-start(f32[4,768,128]{2,1,0:T(8,128)} %bitcast.11), calls=%async_computation | async-start | bytes 3145728 | tf_op jit(solution)/shard_map/all_to_all | solution.py:108
  27.0 0.9 slice_select_fusion
  27.9 4.2 %collective-permute-start.1 = (f32[288,128]{1,0:T(8,128)S(1)}, f32[288,128]{1,0:T(8,128)S(1)}, u32[]{:S(2)}, u32[]{:S(2)}) collective-permute-start(f32[288,128]{1,0:T(8,128)S(1)} %slice_select_fusion), channel_id=1, source_target_pairs={{0,256},{128,384},{256,0},{384,128},{1,257},{129,385},{257,1},{385... | collective-permute-start | bytes 442376 | tf_op jit(solution)/shard_map/ppermute | solution.py:23
  32.8 3.5 %collective-permute-done.1 = f32[288,128]{1,0:T(8,128)S(1)} collective-permute-done((f32[288,128]{1,0:T(8,128)S(1)}, f32[288,128]{1,0:T(8,128)S(1)}, u32[]{:S(2)}, u32[]{:S(2)}) %collective-permute-start.1) | collective-permute-done | bytes 147488 | tf_op jit(solution)/shard_map/ppermute | solution.py:23
  36.3 0.9 reduce_sum.55
  37.2 7.6 %all-to-all-start.1 = ((f32[8,96,128]{2,1,0:T(8,128)}), f32[8,96,128]{2,1,0:T(8,128)S(1)}, u32[]{:S(2)}, u32[]{:S(2)}) async-start(f32[8,96,128]{2,1,0:T(8,128)} %bitcast.12), calls=%async_computation.1 | async-start | bytes 786432 | tf_op jit(solution)/shard_map/all_to_all | solution.py:108
  45.5 2.7 %collective-permute-start.2 = (f32[288,128]{1,0:T(8,128)S(1)}, f32[288,128]{1,0:T(8,128)S(1)}, u32[]{:S(2)}, u32[]{:S(2)}) collective-permute-start(f32[288,128]{1,0:T(8,128)S(1)} %broadcast_select_fusion.1), channel_id=1, source_target_pairs={{0,128},{128,0},{256,384},{384,256},{1,129},{129,1},{257,385},{385... | collective-permute-start | bytes 442376 | tf_op jit(solution)/shard_map/ppermute | solution.py:23
  48.3 3.8 %collective-permute-done.2 = f32[288,128]{1,0:T(8,128)S(1)} collective-permute-done((f32[288,128]{1,0:T(8,128)S(1)}, f32[288,128]{1,0:T(8,128)S(1)}, u32[]{:S(2)}, u32[]{:S(2)}) %collective-permute-start.2) | collective-permute-done | bytes 147488 | tf_op jit(solution)/shard_map/ppermute | solution.py:23
  52.1 2.3 %all-to-all-done.1 = f32[8,96,128]{2,1,0:T(8,128)S(1)} async-done(((f32[8,96,128]{2,1,0:T(8,128)}), f32[8,96,128]{2,1,0:T(8,128)S(1)}, u32[]{:S(2)}, u32[]{:S(2)}) %all-to-all-start.1) | async-done | bytes 393248 | tf_op jit(solution)/shard_map/all_to_all | solution.py:108
  54.4 0.7 fusion
  55.1 0.1 fusion.5
  55.2 0.1 maximum_bitcast_fusion
  55.5 0.1 constant_dynamic-update-slice_fusion.3
  55.7 15.8 %all_to_all.21 = f32[8,48,128]{2,1,0:T(8,128)S(1)} all-to-all(f32[8,48,128]{2,1,0:T(8,128)S(1)} %constant_dynamic-update-slice_fusion), channel_id=1, replica_groups=mesh['yl'=4,'c'=2,'yh'=2,'z'=8,'x'=4] {'yh','yl'}, dimensions={0} | all-to-all | bytes 393216 | tf_op jit(solution)/shard_map/all_to_all | solution.py:118
  71.5 5.2 %all-gather = f32[96,128]{1,0:T(8,128)S(1)} all-gather(f32[48,128]{1,0:T(8,128)S(1)} %reduce_sum.57), channel_id=2, replica_groups=mesh['yl'=4,'c'=2,'yh'=2,'z'=8,'x'=4] {'c'}, dimensions={0}, use_global_device_ids=true | all-gather | bytes 73728 | tf_op jit(solution)/shard_map/all_gather | solution.py:119
  76.9 0.1 slice_bitcast_fusion.7
  77.0 0.1 slice_bitcast_fusion.3
  77.1 0.1 broadcast_in_dim.44
  77.2 0.6 broadcast_in_dim.45
  77.9 6.6 %all-to-all-start.3 = ((f32[64,1,128]{2,1,0:T(1,128)}), f32[64,1,128]{2,1,0:T(1,128)S(1)}, u32[]{:S(2)}, u32[]{:S(2)}) async-start(f32[64,1,128]{2,1,0:T(1,128)} %broadcast_in_dim.45), calls=%async_computation.3 | async-start | bytes 65536 | tf_op jit(solution)/shard_map/all_to_all | solution.py:155
  84.4 0.7 fusion.3
  85.1 0.7 maximum_bitcast_fusion.2
  85.8 0.7 maximum_bitcast_fusion.3
  86.6 0.7 convert_bitcast_fusion
  87.2 10.5 %all-to-all-done.3 = f32[64,1,128]{2,1,0:T(1,128)S(1)} async-done(((f32[64,1,128]{2,1,0:T(1,128)}), f32[64,1,128]{2,1,0:T(1,128)S(1)}, u32[]{:S(2)}, u32[]{:S(2)}) %all-to-all-start.3) | async-done | bytes 32800 | tf_op jit(solution)/shard_map/all_to_all | solution.py:155
  97.7 0.5 reduce_sum.59
  (34 shorter events, 0.7 us)
Async XLA Ops:
  2.1 12.3 %collective-permute-start = (f32[3360,128]{1,0:T(8,128)S(1)}, f32[3360,128]{1,0:T(8,128)}, u32[]{:S(2)}, u32[]{:S(2)}) collective-permute-start(f32[3360,128]{1,0:T(8,128)S(1)} %shard_map.120), channel_id=1, source_target_pairs={{0,64},{64,0},{1,65},{65,1},{2,66},{66,2},{3,67},{67,3},{4,68},{68... | collective-permute-start | bytes 5160968 | tf_op jit(solution)/shard_map/ppermute | solution.py:23
  10.9 2.2 %copy-start.3 = (s32[8]{0:T(128)S(1)}, s32[8]{0:T(128)}, u32[]{:S(2)}) copy-start(s32[8]{0:T(128)} %param.13) | copy-start | bytes 100
  10.9 2.8 %copy-start.5 = (s32[8]{0:T(128)S(1)}, s32[8]{0:T(128)}, u32[]{:S(2)}) copy-start(s32[8]{0:T(128)} %param.14) | copy-start | bytes 100
  17.1 9.9 %copy-start = (f32[1,128,96]{1,2,0:T(8,128)S(1)}, f32[1,128,96]{1,2,0:T(8,128)}, u32[]{:S(2)}) copy-start(f32[1,128,96]{1,2,0:T(8,128)} %param.9) | copy-start | bytes 147460
  17.1 9.9 %copy-start.1 = (f32[1,128,96]{1,2,0:T(8,128)S(1)}, f32[1,128,96]{1,2,0:T(8,128)}, u32[]{:S(2)}) copy-start(f32[1,128,96]{1,2,0:T(8,128)} %param.10) | copy-start | bytes 147460
  17.1 9.9 %copy-start.2 = (f32[1,128,96]{1,2,0:T(8,128)S(1)}, f32[1,128,96]{1,2,0:T(8,128)}, u32[]{:S(2)}) copy-start(f32[1,128,96]{1,2,0:T(8,128)} %param.11) | copy-start | bytes 147460
  17.1 19.3 %all-to-all-start = ((f32[4,768,128]{2,1,0:T(8,128)}), f32[4,768,128]{2,1,0:T(8,128)S(1)}, u32[]{:S(2)}, u32[]{:S(2)}) async-start(f32[4,768,128]{2,1,0:T(8,128)} %bitcast.11), calls=%async_computation | async-start | bytes 3145728 | tf_op jit(solution)/shard_map/all_to_all | solution.py:108
  27.9 8.4 %collective-permute-start.1 = (f32[288,128]{1,0:T(8,128)S(1)}, f32[288,128]{1,0:T(8,128)S(1)}, u32[]{:S(2)}, u32[]{:S(2)}) collective-permute-start(f32[288,128]{1,0:T(8,128)S(1)} %slice_select_fusion), channel_id=1, source_target_pairs={{0,256},{128,384},{256,0},{384,128},{1,257},{129,385},{257,1},{385... | collective-permute-start | bytes 442376 | tf_op jit(solution)/shard_map/ppermute | solution.py:23
  32.8 12.6 %copy-start.4 = (f32[96]{0:T(128)S(1)}, f32[96]{0:T(128)}, u32[]{:S(2)}) copy-start(f32[96]{0:T(128)} %param.12) | copy-start | bytes 1156
  37.2 17.2 %all-to-all-start.1 = ((f32[8,96,128]{2,1,0:T(8,128)}), f32[8,96,128]{2,1,0:T(8,128)S(1)}, u32[]{:S(2)}, u32[]{:S(2)}) async-start(f32[8,96,128]{2,1,0:T(8,128)} %bitcast.12), calls=%async_computation.1 | async-start | bytes 786432 | tf_op jit(solution)/shard_map/all_to_all | solution.py:108
  45.5 6.5 %collective-permute-start.2 = (f32[288,128]{1,0:T(8,128)S(1)}, f32[288,128]{1,0:T(8,128)S(1)}, u32[]{:S(2)}, u32[]{:S(2)}) collective-permute-start(f32[288,128]{1,0:T(8,128)S(1)} %broadcast_select_fusion.1), channel_id=1, source_target_pairs={{0,128},{128,0},{256,384},{384,256},{1,129},{129,1},{257,385},{385... | collective-permute-start | bytes 442376 | tf_op jit(solution)/shard_map/ppermute | solution.py:23
  77.9 19.8 %all-to-all-start.3 = ((f32[64,1,128]{2,1,0:T(1,128)}), f32[64,1,128]{2,1,0:T(1,128)S(1)}, u32[]{:S(2)}, u32[]{:S(2)}) async-start(f32[64,1,128]{2,1,0:T(1,128)} %broadcast_in_dim.45), calls=%async_computation.3 | async-start | bytes 65536 | tf_op jit(solution)/shard_map/all_to_all | solution.py:155

commit v5 on v4

--- a/solution.py
+++ b/solution.py
@@ -141,8 +141,9 @@
     near = jnp.sum(blocks, axis=0).reshape(8, WIDTH, FEAT)
     near, moved = lax.optimization_barrier((near, stage(moved, way, "yl", YL, 2, 4)))
     plane = jnp.sum(exchanged(near, False), axis=0)
-    plane, moved = lax.optimization_barrier((plane, stage(moved, way, "yl", YL, 1, 2)))
-    healed = jnp.where(flagged_here, moved, state).reshape(3, WIDTH, FEAT)
+    moved = stage(moved, way, "yl", YL, 1, 2)
+    plane, healed = lax.optimization_barrier((plane, jnp.where(flagged_here, moved, state)))
+    healed = healed.reshape(3, WIDTH, FEAT)
     packed = jnp.stack([two_up(healed, half) for half in range(C)])
     upper = lax.broadcasted_iota(jnp.int32, (ROWS, FEAT), 1) < HALF
     weights = jnp.where(upper, probe[:ROWS, None], probe[ROWS:, None])

time: 98.9 us -> 98.3 us (level)
  transfers between devices with their start and end apart: 6 -> 6, of which waited for: 4 -> 4; matrix products, arithmetic and copies ran while one was open for 5% -> 6% of each run, Pallas kernels for 1% -> 1%
where the time goes in v5:
time: 98.3 us; the launch traced here: 97.7 us
  starting transfers between devices  39.1 us (40%)
  blocking collectives  21.1 us (21%)
  waiting for transfers between devices  19.4 us (20%)
  other arithmetic  10.4 us (11%)
  between operations  3.54 us (4%)
  Pallas kernels  2.87 us (3%)
  local copies, waits for them, and re-layouts  1.27 us (1%)
    all_to_all x2, starting transfers between devices, exchanged(): lax.all_to_all(blocks, every, 0, 0, tiled=True, axis_index_groups=groups(...  16.8 us
    all_to_all x1, blocking collectives, line_grad(): lines = lax.all_to_all(spread, ('yh', 'yl'), 0, 0, tiled=True)  15.8 us
    ppermute x3, starting transfers between devices, swapped(): return lax.ppermute(value, axis, [(i, i ^ bit) for i in range(size)])  15.7 us
    all_to_all x1, waiting for transfers between devices, shards(): checksum = jnp.sum(lax.all_to_all(spread, FSDP, 0, 0, tiled=True), axis=0)  10.5 us
    ppermute x3, waiting for transfers between devices, swapped(): return lax.ppermute(value, axis, [(i, i ^ bit) for i in range(size)])  7.27 us
    all_to_all x1, starting transfers between devices, shards(): checksum = jnp.sum(lax.all_to_all(spread, FSDP, 0, 0, tiled=True), axis=0)  6.62 us
    all_gather x1, blocking collectives, line_grad(): return lax.all_gather(jnp.sum(lines, axis=0), 'c', axis=0, tiled=False)  5.24 us
    pallas_call x2, Pallas kernels, turned(): pl.pallas_call(give_kernel if state else turn_kernel, grid_spec=pltpu.Pre...  2.87 us
  transfers between devices with their start and end apart: 6, of which 4 were waited for; matrix products, arithmetic and copies ran while one was open for 6% of the time, Pallas kernels for 1%

profile of v5, /device:TPU:1, one launch (start us, length us, event | category | flops | bytes accessed | tf_op | source)
XLA Modules:
  0.0 97.7 jit_solution(8705223705449017767)
XLA Ops:
  0.6 1.5 %shard_map.120 = f32[3360,128]{1,0:T(8,128)S(1)} custom-call(s32[1]{0:T(128)} %bitcast.4.half_ref, bf16[128,6144]{1,0:T(8,128)(2,1)} %bitcast.89, f32[96,128]{1,0:T(8,128)} %bitcast.92, f32[96,128]{1,0:T(8,128)} %bitcast.95, f32[96,128]{1,0:T(8,128)} %bitcast.98), custom_call_target="tpu_custom_call" | custom-call | bytes 2359296 | tf_op jit(solution)/shard_map/pallas_call | solution.py:73
  2.1 8.8 %collective-permute-start = (f32[3360,128]{1,0:T(8,128)S(1)}, f32[3360,128]{1,0:T(8,128)}, u32[]{:S(2)}, u32[]{:S(2)}) collective-permute-start(f32[3360,128]{1,0:T(8,128)S(1)} %shard_map.120), channel_id=1, source_target_pairs={{0,64},{64,0},{1,65},{65,1},{2,66},{66,2},{3,67},{67,3},{4,68},{68... | collective-permute-start | bytes 5160968 | tf_op jit(solution)/shard_map/ppermute | solution.py:23
  10.9 1.4 %shard_map.119 = f32[3072,128]{1,0:T(8,128)S(1)} custom-call(s32[1]{0:T(128)} %bitcast.half_ref, bf16[128,6144]{1,0:T(8,128)(2,1)} %bitcast.90), custom_call_target="tpu_custom_call" | custom-call | bytes 2359296 | tf_op jit(solution)/shard_map/pallas_call | solution.py:73
  13.1 0.6 and_reduce_fusion
  13.7 0.6 fusion.3
  14.4 2.7 %slice_add_fusion = f32[3072,128]{1,0:T(8,128)} fusion(f32[3072,128]{1,0:T(8,128)S(1)} %shard_map.119, f32[3360,128]{1,0:T(8,128)} %collective-permute-done), kind=kLoop, calls=%fused_computation | loop fusion | flops 393216 | bytes 4718592 | tf_op jit(solution)/shard_map/add | solution.py:93
  17.1 9.2 %all-to-all-start = ((f32[4,768,128]{2,1,0:T(8,128)}), f32[4,768,128]{2,1,0:T(8,128)S(1)}, u32[]{:S(2)}, u32[]{:S(2)}) async-start(f32[4,768,128]{2,1,0:T(8,128)} %bitcast.11), calls=%async_computation | async-start | bytes 3145728 | tf_op jit(solution)/shard_map/all_to_all | solution.py:108
  27.0 0.9 slice_select_fusion
  27.9 4.2 %collective-permute-start.1 = (f32[288,128]{1,0:T(8,128)S(1)}, f32[288,128]{1,0:T(8,128)S(1)}, u32[]{:S(2)}, u32[]{:S(2)}) collective-permute-start(f32[288,128]{1,0:T(8,128)S(1)} %slice_select_fusion), channel_id=1, source_target_pairs={{0,256},{128,384},{256,0},{384,128},{1,257},{129,385},{257,1},{385... | collective-permute-start | bytes 442376 | tf_op jit(solution)/shard_map/ppermute | solution.py:23
  32.8 3.5 %collective-permute-done.1 = f32[288,128]{1,0:T(8,128)S(1)} collective-permute-done((f32[288,128]{1,0:T(8,128)S(1)}, f32[288,128]{1,0:T(8,128)S(1)}, u32[]{:S(2)}, u32[]{:S(2)}) %collective-permute-start.1) | collective-permute-done | bytes 147488 | tf_op jit(solution)/shard_map/ppermute | solution.py:23
  36.3 0.9 reduce_sum.55
  37.2 7.6 %all-to-all-start.1 = ((f32[8,96,128]{2,1,0:T(8,128)}), f32[8,96,128]{2,1,0:T(8,128)S(1)}, u32[]{:S(2)}, u32[]{:S(2)}) async-start(f32[8,96,128]{2,1,0:T(8,128)} %bitcast.12), calls=%async_computation.1 | async-start | bytes 786432 | tf_op jit(solution)/shard_map/all_to_all | solution.py:108
  45.5 2.7 %collective-permute-start.2 = (f32[288,128]{1,0:T(8,128)S(1)}, f32[288,128]{1,0:T(8,128)S(1)}, u32[]{:S(2)}, u32[]{:S(2)}) collective-permute-start(f32[288,128]{1,0:T(8,128)S(1)} %broadcast_select_fusion), channel_id=1, source_target_pairs={{0,128},{128,0},{256,384},{384,256},{1,129},{129,1},{257,385},{385... | collective-permute-start | bytes 442376 | tf_op jit(solution)/shard_map/ppermute | solution.py:23
  48.3 3.8 %collective-permute-done.2 = f32[288,128]{1,0:T(8,128)S(1)} collective-permute-done((f32[288,128]{1,0:T(8,128)S(1)}, f32[288,128]{1,0:T(8,128)S(1)}, u32[]{:S(2)}, u32[]{:S(2)}) %collective-permute-start.2) | collective-permute-done | bytes 147488 | tf_op jit(solution)/shard_map/ppermute | solution.py:23
  52.1 0.7 select_select_fusion
  52.7 1.7 %all-to-all-done.1 = f32[8,96,128]{2,1,0:T(8,128)S(1)} async-done(((f32[8,96,128]{2,1,0:T(8,128)}), f32[8,96,128]{2,1,0:T(8,128)S(1)}, u32[]{:S(2)}, u32[]{:S(2)}) %all-to-all-start.1) | async-done | bytes 393248 | tf_op jit(solution)/shard_map/all_to_all | solution.py:108
  54.4 0.1 fusion.4
  54.6 0.1 maximum_bitcast_fusion
  54.9 0.1 constant_dynamic-update-slice_fusion.3
  55.0 15.8 %all_to_all.21 = f32[8,48,128]{2,1,0:T(8,128)S(1)} all-to-all(f32[8,48,128]{2,1,0:T(8,128)S(1)} %constant_dynamic-update-slice_fusion), channel_id=1, replica_groups=mesh['yl'=4,'c'=2,'yh'=2,'z'=8,'x'=4] {'yh','yl'}, dimensions={0} | all-to-all | bytes 393216 | tf_op jit(solution)/shard_map/all_to_all | solution.py:118
  70.8 5.2 %all-gather = f32[96,128]{1,0:T(8,128)S(1)} all-gather(f32[48,128]{1,0:T(8,128)S(1)} %reduce_sum.57), channel_id=2, replica_groups=mesh['yl'=4,'c'=2,'yh'=2,'z'=8,'x'=4] {'c'}, dimensions={0}, use_global_device_ids=true | all-gather | bytes 73728 | tf_op jit(solution)/shard_map/all_gather | solution.py:119
  76.2 0.1 slice_bitcast_fusion.7
  76.3 0.1 slice_bitcast_fusion.3
  76.5 0.1 broadcast_in_dim.44
  76.6 0.6 broadcast_in_dim.45
  77.2 6.6 %all-to-all-start.3 = ((f32[64,1,128]{2,1,0:T(1,128)}), f32[64,1,128]{2,1,0:T(1,128)S(1)}, u32[]{:S(2)}, u32[]{:S(2)}) async-start(f32[64,1,128]{2,1,0:T(1,128)} %broadcast_in_dim.45), calls=%async_computation.3 | async-start | bytes 65536 | tf_op jit(solution)/shard_map/all_to_all | solution.py:156
  83.8 0.7 fusion.2
  84.5 0.7 maximum_bitcast_fusion.2
  85.2 0.7 maximum_bitcast_fusion.3
  85.9 0.7 convert_bitcast_fusion
  86.6 10.5 %all-to-all-done.3 = f32[64,1,128]{2,1,0:T(1,128)S(1)} async-done(((f32[64,1,128]{2,1,0:T(1,128)}), f32[64,1,128]{2,1,0:T(1,128)S(1)}, u32[]{:S(2)}, u32[]{:S(2)}) %all-to-all-start.3) | async-done | bytes 32800 | tf_op jit(solution)/shard_map/all_to_all | solution.py:156
  97.1 0.5 reduce_sum.59
  (33 shorter events, 0.7 us)
Async XLA Ops:
  2.1 12.3 %collective-permute-start = (f32[3360,128]{1,0:T(8,128)S(1)}, f32[3360,128]{1,0:T(8,128)}, u32[]{:S(2)}, u32[]{:S(2)}) collective-permute-start(f32[3360,128]{1,0:T(8,128)S(1)} %shard_map.120), channel_id=1, source_target_pairs={{0,64},{64,0},{1,65},{65,1},{2,66},{66,2},{3,67},{67,3},{4,68},{68... | collective-permute-start | bytes 5160968 | tf_op jit(solution)/shard_map/ppermute | solution.py:23
  10.9 2.2 %copy-start.3 = (s32[8]{0:T(128)S(1)}, s32[8]{0:T(128)}, u32[]{:S(2)}) copy-start(s32[8]{0:T(128)} %param.13) | copy-start | bytes 100
  10.9 2.8 %copy-start.5 = (s32[8]{0:T(128)S(1)}, s32[8]{0:T(128)}, u32[]{:S(2)}) copy-start(s32[8]{0:T(128)} %param.14) | copy-start | bytes 100
  17.1 9.9 %copy-start = (f32[1,128,96]{1,2,0:T(8,128)S(1)}, f32[1,128,96]{1,2,0:T(8,128)}, u32[]{:S(2)}) copy-start(f32[1,128,96]{1,2,0:T(8,128)} %param.9) | copy-start | bytes 147460
  17.1 9.9 %copy-start.1 = (f32[1,128,96]{1,2,0:T(8,128)S(1)}, f32[1,128,96]{1,2,0:T(8,128)}, u32[]{:S(2)}) copy-start(f32[1,128,96]{1,2,0:T(8,128)} %param.10) | copy-start | bytes 147460
  17.1 9.9 %copy-start.2 = (f32[1,128,96]{1,2,0:T(8,128)S(1)}, f32[1,128,96]{1,2,0:T(8,128)}, u32[]{:S(2)}) copy-start(f32[1,128,96]{1,2,0:T(8,128)} %param.11) | copy-start | bytes 147460
  17.1 19.3 %all-to-all-start = ((f32[4,768,128]{2,1,0:T(8,128)}), f32[4,768,128]{2,1,0:T(8,128)S(1)}, u32[]{:S(2)}, u32[]{:S(2)}) async-start(f32[4,768,128]{2,1,0:T(8,128)} %bitcast.11), calls=%async_computation | async-start | bytes 3145728 | tf_op jit(solution)/shard_map/all_to_all | solution.py:108
  27.9 8.4 %collective-permute-start.1 = (f32[288,128]{1,0:T(8,128)S(1)}, f32[288,128]{1,0:T(8,128)S(1)}, u32[]{:S(2)}, u32[]{:S(2)}) collective-permute-start(f32[288,128]{1,0:T(8,128)S(1)} %slice_select_fusion), channel_id=1, source_target_pairs={{0,256},{128,384},{256,0},{384,128},{1,257},{129,385},{257,1},{385... | collective-permute-start | bytes 442376 | tf_op jit(solution)/shard_map/ppermute | solution.py:23
  32.8 12.6 %copy-start.4 = (f32[96]{0:T(128)S(1)}, f32[96]{0:T(128)}, u32[]{:S(2)}) copy-start(f32[96]{0:T(128)} %param.12) | copy-start | bytes 1156
  37.2 17.2 %all-to-all-start.1 = ((f32[8,96,128]{2,1,0:T(8,128)}), f32[8,96,128]{2,1,0:T(8,128)S(1)}, u32[]{:S(2)}, u32[]{:S(2)}) async-start(f32[8,96,128]{2,1,0:T(8,128)} %bitcast.12), calls=%async_computation.1 | async-start | bytes 786432 | tf_op jit(solution)/shard_map/all_to_all | solution.py:108
  45.5 6.5 %collective-permute-start.2 = (f32[288,128]{1,0:T(8,128)S(1)}, f32[288,128]{1,0:T(8,128)S(1)}, u32[]{:S(2)}, u32[]{:S(2)}) collective-permute-start(f32[288,128]{1,0:T(8,128)S(1)} %broadcast_select_fusion), channel_id=1, source_target_pairs={{0,128},{128,0},{256,384},{384,256},{1,129},{129,1},{257,385},{385... | collective-permute-start | bytes 442376 | tf_op jit(solution)/shard_map/ppermute | solution.py:23
  77.2 19.9 %all-to-all-start.3 = ((f32[64,1,128]{2,1,0:T(1,128)}), f32[64,1,128]{2,1,0:T(1,128)S(1)}, u32[]{:S(2)}, u32[]{:S(2)}) async-start(f32[64,1,128]{2,1,0:T(1,128)} %broadcast_in_dim.45), calls=%async_computation.3 | async-start | bytes 65536 | tf_op jit(solution)/shard_map/all_to_all | solution.py:156

commit v6 on v5

--- a/solution.py
+++ b/solution.py
@@ -38,33 +38,60 @@
     return (new_master, new_first, new_second)
 
 
-def give_kernel(half_ref, grad_ref, master_ref, first_ref, second_ref, turned_ref):
-    turn_kernel(half_ref, grad_ref, turned_ref)
-    start = Z * X * WIDTH
-    for i, state_ref in enumerate((master_ref, first_ref, second_ref)):
-        turned_ref[start + i * WIDTH : start + (i + 1) * WIDTH, :] = state_ref[...]
-
-
 def near_place(core, z, x):
     z, x = (z - core) % Z, (x - core) % X
     return z % 2 * 2 + x % 2, z // 2 * 2 + x // 2
 
 
+def turn_columns(half, zs, grad_ref, turned_ref):
+    columns = Z * X * WIDTH
+    wide = X * WIDTH
+    for z in zs:
+        first = grad_ref[:, z * wide : (z + 1) * wide]
+        second = grad_ref[:, columns + z * wide : columns + (z + 1) * wide]
+        value = jnp.concatenate([first, second], axis=0).T.astype(jnp.float32)
+        for x in range(X):
+            near, far = near_place(half, z, x)
+            row = (near * 8 + far) * WIDTH
+            turned_ref[row : row + WIDTH, :] = value[x * WIDTH : (x + 1) * WIDTH]
+
+
 def turn_kernel(half_ref, grad_ref, turned_ref):
-    columns = Z * X * WIDTH
-    wide = X * WIDTH
     for half in range(C):
 
         @pl.when(half_ref[0] == half)
         def _():
-            for z in range(Z):
-                first = grad_ref[:, z * wide : (z + 1) * wide]
-                second = grad_ref[:, columns + z * wide : columns + (z + 1) * wide]
-                value = jnp.concatenate([first, second], axis=0).T.astype(jnp.float32)
-                for x in range(X):
-                    near, far = near_place(half, z, x)
-                    row = (near * 8 + far) * WIDTH
-                    turned_ref[row : row + WIDTH, :] = value[x * WIDTH : (x + 1) * WIDTH]
+            turn_columns(half, range(Z), grad_ref, turned_ref)
+
+
+def give_kernel(half_ref, grad_ref, master_ref, first_ref, second_ref, out_ref, turned_ref, sems):
+    columns = Z * X * WIDTH
+    states = [
+        pltpu.make_async_copy(
+            ref, out_ref.at[pl.ds(columns + i * WIDTH, WIDTH)], sems.at[2 + i]
+        )
+        for i, ref in enumerate((master_ref, first_ref, second_ref))
+    ]
+    for copy in states:
+        copy.start()
+    for half in range(C):
+
+        @pl.when(half_ref[0] == half)
+        def _():
+            parts = []
+            for part in range(2):
+                zs = [(2 * i + part + half) % Z for i in range(Z // 2)]
+                turn_columns(half, zs, grad_ref, turned_ref)
+                rows = pl.ds(part * columns // 2, columns // 2)
+                parts.append(
+                    pltpu.make_async_copy(turned_ref.at[rows], out_ref.at[rows], sems.at[part])
+                )
+                parts[part].start()
+            for copy in parts:
+                copy.wait()
+
+    for copy in states:
+        copy.wait()
 
 
 def turned(grad, half, *state):
@@ -77,9 +104,12 @@
             grid=(1,),
             in_specs=[pl.BlockSpec((HALF, YH * columns), lambda i, half_ref: (half_ref[0], 0))]
             + [pl.BlockSpec((WIDTH, FEAT), lambda i, half_ref: (0, 0))] * len(state),
-            out_specs=pl.BlockSpec(memory_space=pltpu.VMEM),
+            out_specs=pl.BlockSpec(memory_space=pl.ANY if state else pltpu.VMEM),
+            scratch_shapes=[pltpu.VMEM((columns, FEAT), jnp.float32), pltpu.SemaphoreType.DMA((5,))]
+            if state
+            else [],
         ),
-        out_shape=pltpu.VMEM((rows, FEAT), jnp.float32),
+        out_shape=(jax.ShapeDtypeStruct if state else pltpu.VMEM)((rows, FEAT), jnp.float32),
         cost_estimate=pl.CostEstimate(flops=0, bytes_accessed=columns * FEAT * 6, transcendentals=0),
     )(half.reshape(1), grad, *state)
 

time: 98.3 us -> 98 us (level)
  other arithmetic: 10.4 us -> 8.85 us
  Pallas kernels: 2.87 us -> 3.96 us
    add x1, other arithmetic: 2.7 us -> 1.31 us  [chip_sum(): return (kept + given[:columns], given[columns:], *beside)]
    pallas_call x2, Pallas kernels: 2.87 us -> 3.96 us  [turned(): pl.pallas_call(give_kernel if state else turn_kernel, grid_spec=pltpu.Pre...]
where the time goes in v6:
time: 98 us; the launch traced here: 97.3 us
  starting transfers between devices  39.2 us (40%)
  blocking collectives  21 us (21%)
  waiting for transfers between devices  19.5 us (20%)
  other arithmetic  8.85 us (9%)
  Pallas kernels  3.96 us (4%)
  between operations  3.53 us (4%)
  local copies, waits for them, and re-layouts  1.27 us (1%)
    all_to_all x2, starting transfers between devices, exchanged(): lax.all_to_all(blocks, every, 0, 0, tiled=True, axis_index_groups=groups(...  16.9 us
    ppermute x3, starting transfers between devices, swapped(): return lax.ppermute(value, axis, [(i, i ^ bit) for i in range(size)])  15.7 us
    all_to_all x1, blocking collectives, line_grad(): lines = lax.all_to_all(spread, ('yh', 'yl'), 0, 0, tiled=True)  15.7 us
    all_to_all x1, waiting for transfers between devices, shards(): checksum = jnp.sum(lax.all_to_all(spread, FSDP, 0, 0, tiled=True), axis=0)  10.5 us
    ppermute x3, waiting for transfers between devices, swapped(): return lax.ppermute(value, axis, [(i, i ^ bit) for i in range(size)])  7.34 us
    all_to_all x1, starting transfers between devices, shards(): checksum = jnp.sum(lax.all_to_all(spread, FSDP, 0, 0, tiled=True), axis=0)  6.62 us
    all_gather x1, blocking collectives, line_grad(): return lax.all_gather(jnp.sum(lines, axis=0), 'c', axis=0, tiled=False)  5.3 us
    pallas_call x2, Pallas kernels, turned(): pl.pallas_call(give_kernel if state else turn_kernel, grid_spec=pltpu.Pre...  3.96 us
  transfers between devices with their start and end apart: 6, of which 4 were waited for; matrix products, arithmetic and copies ran while one was open for 6% of the time, Pallas kernels for 1%

profile of v6, /device:TPU:1, one launch (start us, length us, event | category | flops | bytes accessed | tf_op | source)
XLA Modules:
  0.0 97.3 jit_solution(7425630427865797036)
XLA Ops:
  0.6 2.6 %shard_map.120 = f32[3360,128]{1,0:T(8,128)} custom-call(s32[1]{0:T(128)} %bitcast.4.half_ref, bf16[128,6144]{1,0:T(8,128)(2,1)} %bitcast.89, f32[96,128]{1,0:T(8,128)} %bitcast.92, f32[96,128]{1,0:T(8,128)} %bitcast.95, f32[96,128]{1,0:T(8,128)} %bitcast.98), custom_call_target="tpu_custom_call" | custom-call | bytes 2359296 | tf_op jit(solution)/shard_map/pallas_call | solution.py:100
  3.2 8.8 %collective-permute-start = (f32[3360,128]{1,0:T(8,128)}, f32[3360,128]{1,0:T(8,128)S(1)}, u32[]{:S(2)}, u32[]{:S(2)}) collective-permute-start(f32[3360,128]{1,0:T(8,128)} %shard_map.120), channel_id=1, source_target_pairs={{0,64},{64,0},{1,65},{65,1},{2,66},{66,2},{3,67},{67,3},{4,68},{68... | collective-permute-start | bytes 5160968 | tf_op jit(solution)/shard_map/ppermute | solution.py:23
  12.0 1.4 %shard_map.119 = f32[3072,128]{1,0:T(8,128)S(1)} custom-call(s32[1]{0:T(128)} %bitcast.half_ref, bf16[128,6144]{1,0:T(8,128)(2,1)} %bitcast.90), custom_call_target="tpu_custom_call" | custom-call | bytes 2359296 | tf_op jit(solution)/shard_map/pallas_call | solution.py:100
  14.2 0.6 and_reduce_fusion
  14.8 0.6 fusion.3
  15.5 1.3 %slice_add_fusion = f32[3072,128]{1,0:T(8,128)} fusion(f32[3072,128]{1,0:T(8,128)S(1)} %shard_map.119, f32[3360,128]{1,0:T(8,128)S(1)} %collective-permute-done), kind=kLoop, calls=%fused_computation | loop fusion | flops 393216 | bytes 4718592 | tf_op jit(solution)/shard_map/add | solution.py:123
  16.8 9.2 %all-to-all-start = ((f32[4,768,128]{2,1,0:T(8,128)}), f32[4,768,128]{2,1,0:T(8,128)S(1)}, u32[]{:S(2)}, u32[]{:S(2)}) async-start(f32[4,768,128]{2,1,0:T(8,128)} %bitcast.11), calls=%async_computation | async-start | bytes 3145728 | tf_op jit(solution)/shard_map/all_to_all | solution.py:138
  26.7 0.8 slice_select_fusion
  27.5 4.2 %collective-permute-start.1 = (f32[288,128]{1,0:T(8,128)S(1)}, f32[288,128]{1,0:T(8,128)S(1)}, u32[]{:S(2)}, u32[]{:S(2)}) collective-permute-start(f32[288,128]{1,0:T(8,128)S(1)} %slice_select_fusion), channel_id=1, source_target_pairs={{0,256},{128,384},{256,0},{384,128},{1,257},{129,385},{257,1},{385... | collective-permute-start | bytes 442376 | tf_op jit(solution)/shard_map/ppermute | solution.py:23
  32.4 3.5 %collective-permute-done.1 = f32[288,128]{1,0:T(8,128)S(1)} collective-permute-done((f32[288,128]{1,0:T(8,128)S(1)}, f32[288,128]{1,0:T(8,128)S(1)}, u32[]{:S(2)}, u32[]{:S(2)}) %collective-permute-start.1) | collective-permute-done | bytes 147488 | tf_op jit(solution)/shard_map/ppermute | solution.py:23
  35.9 0.9 reduce_sum.55
  36.8 7.6 %all-to-all-start.1 = ((f32[8,96,128]{2,1,0:T(8,128)}), f32[8,96,128]{2,1,0:T(8,128)S(1)}, u32[]{:S(2)}, u32[]{:S(2)}) async-start(f32[8,96,128]{2,1,0:T(8,128)} %bitcast.12), calls=%async_computation.1 | async-start | bytes 786432 | tf_op jit(solution)/shard_map/all_to_all | solution.py:138
  45.2 2.7 %collective-permute-start.2 = (f32[288,128]{1,0:T(8,128)S(1)}, f32[288,128]{1,0:T(8,128)S(1)}, u32[]{:S(2)}, u32[]{:S(2)}) collective-permute-start(f32[288,128]{1,0:T(8,128)S(1)} %broadcast_select_fusion), channel_id=1, source_target_pairs={{0,128},{128,0},{256,384},{384,256},{1,129},{129,1},{257,385},{385... | collective-permute-start | bytes 442376 | tf_op jit(solution)/shard_map/ppermute | solution.py:23
  47.9 3.9 %collective-permute-done.2 = f32[288,128]{1,0:T(8,128)S(1)} collective-permute-done((f32[288,128]{1,0:T(8,128)S(1)}, f32[288,128]{1,0:T(8,128)S(1)}, u32[]{:S(2)}, u32[]{:S(2)}) %collective-permute-start.2) | collective-permute-done | bytes 147488 | tf_op jit(solution)/shard_map/ppermute | solution.py:23
  51.8 0.7 select_select_fusion
  52.5 1.7 %all-to-all-done.1 = f32[8,96,128]{2,1,0:T(8,128)S(1)} async-done(((f32[8,96,128]{2,1,0:T(8,128)}), f32[8,96,128]{2,1,0:T(8,128)S(1)}, u32[]{:S(2)}, u32[]{:S(2)}) %all-to-all-start.1) | async-done | bytes 393248 | tf_op jit(solution)/shard_map/all_to_all | solution.py:138
  54.2 0.1 fusion.4
  54.3 0.1 maximum_bitcast_fusion
  54.6 0.1 constant_dynamic-update-slice_fusion.3
  54.7 15.7 %all_to_all.21 = f32[8,48,128]{2,1,0:T(8,128)S(1)} all-to-all(f32[8,48,128]{2,1,0:T(8,128)S(1)} %constant_dynamic-update-slice_fusion), channel_id=1, replica_groups=mesh['yl'=4,'c'=2,'yh'=2,'z'=8,'x'=4] {'yh','yl'}, dimensions={0} | all-to-all | bytes 393216 | tf_op jit(solution)/shard_map/all_to_all | solution.py:148
  70.4 5.3 %all-gather = f32[96,128]{1,0:T(8,128)S(1)} all-gather(f32[48,128]{1,0:T(8,128)S(1)} %reduce_sum.57), channel_id=2, replica_groups=mesh['yl'=4,'c'=2,'yh'=2,'z'=8,'x'=4] {'c'}, dimensions={0}, use_global_device_ids=true | all-gather | bytes 73728 | tf_op jit(solution)/shard_map/all_gather | solution.py:149
  75.9 0.1 slice_bitcast_fusion.7
  76.0 0.1 slice_bitcast_fusion.3
  76.1 0.1 broadcast_in_dim.44
  76.2 0.6 broadcast_in_dim.45
  76.9 6.6 %all-to-all-start.3 = ((f32[64,1,128]{2,1,0:T(1,128)}), f32[64,1,128]{2,1,0:T(1,128)S(1)}, u32[]{:S(2)}, u32[]{:S(2)}) async-start(f32[64,1,128]{2,1,0:T(1,128)} %broadcast_in_dim.45), calls=%async_computation.3 | async-start | bytes 65536 | tf_op jit(solution)/shard_map/all_to_all | solution.py:186
  83.5 0.7 fusion.2
  84.2 0.7 maximum_bitcast_fusion.2
  84.9 0.7 maximum_bitcast_fusion.3
  85.6 0.7 convert_bitcast_fusion
  86.3 10.5 %all-to-all-done.3 = f32[64,1,128]{2,1,0:T(1,128)S(1)} async-done(((f32[64,1,128]{2,1,0:T(1,128)}), f32[64,1,128]{2,1,0:T(1,128)S(1)}, u32[]{:S(2)}, u32[]{:S(2)}) %all-to-all-start.3) | async-done | bytes 32800 | tf_op jit(solution)/shard_map/all_to_all | solution.py:186
  96.8 0.5 reduce_sum.59
  (33 shorter events, 0.7 us)
Async XLA Ops:
  3.2 12.3 %collective-permute-start = (f32[3360,128]{1,0:T(8,128)}, f32[3360,128]{1,0:T(8,128)S(1)}, u32[]{:S(2)}, u32[]{:S(2)}) collective-permute-start(f32[3360,128]{1,0:T(8,128)} %shard_map.120), channel_id=1, source_target_pairs={{0,64},{64,0},{1,65},{65,1},{2,66},{66,2},{3,67},{67,3},{4,68},{68... | collective-permute-start | bytes 5160968 | tf_op jit(solution)/shard_map/ppermute | solution.py:23
  12.0 2.2 %copy-start.3 = (s32[8]{0:T(128)S(1)}, s32[8]{0:T(128)}, u32[]{:S(2)}) copy-start(s32[8]{0:T(128)} %param.13) | copy-start | bytes 100
  12.0 2.8 %copy-start.5 = (s32[8]{0:T(128)S(1)}, s32[8]{0:T(128)}, u32[]{:S(2)}) copy-start(s32[8]{0:T(128)} %param.14) | copy-start | bytes 100
  16.8 9.9 %copy-start = (f32[1,128,96]{1,2,0:T(8,128)S(1)}, f32[1,128,96]{1,2,0:T(8,128)}, u32[]{:S(2)}) copy-start(f32[1,128,96]{1,2,0:T(8,128)} %param.9) | copy-start | bytes 147460
  16.8 9.9 %copy-start.1 = (f32[1,128,96]{1,2,0:T(8,128)S(1)}, f32[1,128,96]{1,2,0:T(8,128)}, u32[]{:S(2)}) copy-start(f32[1,128,96]{1,2,0:T(8,128)} %param.10) | copy-start | bytes 147460
  16.8 19.1 %all-to-all-start = ((f32[4,768,128]{2,1,0:T(8,128)}), f32[4,768,128]{2,1,0:T(8,128)S(1)}, u32[]{:S(2)}, u32[]{:S(2)}) async-start(f32[4,768,128]{2,1,0:T(8,128)} %bitcast.11), calls=%async_computation | async-start | bytes 3145728 | tf_op jit(solution)/shard_map/all_to_all | solution.py:138
  27.5 8.4 %collective-permute-start.1 = (f32[288,128]{1,0:T(8,128)S(1)}, f32[288,128]{1,0:T(8,128)S(1)}, u32[]{:S(2)}, u32[]{:S(2)}) collective-permute-start(f32[288,128]{1,0:T(8,128)S(1)} %slice_select_fusion), channel_id=1, source_target_pairs={{0,256},{128,384},{256,0},{384,128},{1,257},{129,385},{257,1},{385... | collective-permute-start | bytes 442376 | tf_op jit(solution)/shard_map/ppermute | solution.py:23
  32.4 12.7 %copy-start.4 = (f32[96]{0:T(128)S(1)}, f32[96]{0:T(128)}, u32[]{:S(2)}) copy-start(f32[96]{0:T(128)} %param.12) | copy-start | bytes 1156
  32.4 19.4 %copy-start.2 = (f32[1,128,96]{1,2,0:T(8,128)S(1)}, f32[1,128,96]{1,2,0:T(8,128)}, u32[]{:S(2)}) copy-start(f32[1,128,96]{1,2,0:T(8,128)} %param.11) | copy-start | bytes 147460
  36.8 17.4 %all-to-all-start.1 = ((f32[8,96,128]{2,1,0:T(8,128)}), f32[8,96,128]{2,1,0:T(8,128)S(1)}, u32[]{:S(2)}, u32[]{:S(2)}) async-start(f32[8,96,128]{2,1,0:T(8,128)} %bitcast.12), calls=%async_computation.1 | async-start | bytes 786432 | tf_op jit(solution)/shard_map/all_to_all | solution.py:138
  45.2 6.6 %collective-permute-start.2 = (f32[288,128]{1,0:T(8,128)S(1)}, f32[288,128]{1,0:T(8,128)S(1)}, u32[]{:S(2)}, u32[]{:S(2)}) collective-permute-start(f32[288,128]{1,0:T(8,128)S(1)} %broadcast_select_fusion), channel_id=1, source_target_pairs={{0,128},{128,0},{256,384},{384,256},{1,129},{129,1},{257,385},{385... | collective-permute-start | bytes 442376 | tf_op jit(solution)/shard_map/ppermute | solution.py:23
  76.9 19.9 %all-to-all-start.3 = ((f32[64,1,128]{2,1,0:T(1,128)}), f32[64,1,128]{2,1,0:T(1,128)S(1)}, u32[]{:S(2)}, u32[]{:S(2)}) async-start(f32[64,1,128]{2,1,0:T(1,128)} %broadcast_in_dim.45), calls=%async_computation.3 | async-start | bytes 65536 | tf_op jit(solution)/shard_map/all_to_all | solution.py:186

commit v7 on v6

--- a/solution.py
+++ b/solution.py
@@ -169,11 +169,15 @@
     moved = jnp.where((way & 1) != 0, other, state)
     blocks = exchanged(chip.reshape(4, 8 * WIDTH, FEAT), True)
     near = jnp.sum(blocks, axis=0).reshape(8, WIDTH, FEAT)
-    near, moved = lax.optimization_barrier((near, stage(moved, way, "yl", YL, 2, 4)))
+    cut = 3 * WIDTH // 2
+    first = stage(moved[:cut], way, "yl", YL, 2, 4)
+    second = stage(moved[cut:], way, "yl", YL, 1, 2)
+    near, first, second = lax.optimization_barrier((near, first, second))
     plane = jnp.sum(exchanged(near, False), axis=0)
-    moved = stage(moved, way, "yl", YL, 1, 2)
-    plane, healed = lax.optimization_barrier((plane, jnp.where(flagged_here, moved, state)))
-    healed = healed.reshape(3, WIDTH, FEAT)
+    first = jnp.where(flagged_here, stage(first, way, "yl", YL, 1, 2), state[:cut])
+    second = jnp.where(flagged_here, stage(second, way, "yl", YL, 2, 4), state[cut:])
+    plane, first, second = lax.optimization_barrier((plane, first, second))
+    healed = jnp.concatenate([first, second]).reshape(3, WIDTH, FEAT)
     packed = jnp.stack([two_up(healed, half) for half in range(C)])
     upper = lax.broadcasted_iota(jnp.int32, (ROWS, FEAT), 1) < HALF
     weights = jnp.where(upper, probe[:ROWS, None], probe[ROWS:, None])

time: 98 us -> 98.8 us (level)
  starting transfers between devices: 39.2 us -> 46.4 us
  waiting for transfers between devices: 19.5 us -> 14.4 us
  blocking collectives: 21 us -> 19.6 us
    ppermute x3 -> x5, starting transfers between devices: 15.7 us -> 22.8 us  [swapped(): return lax.ppermute(value, axis, [(i, i ^ bit) for i in range(size)])]
    ppermute x3 -> x5, waiting for transfers between devices: 7.34 us -> 3.41 us  [swapped(): return lax.ppermute(value, axis, [(i, i ^ bit) for i in range(size)])]
    all_to_all x1, blocking collectives: 15.7 us -> 14.2 us  [line_grad(): lines = lax.all_to_all(spread, ('yh', 'yl'), 0, 0, tiled=True)]
    all_to_all x1, starting transfers between devices: 6.62 us -> 7.94 us  [shards(): checksum = jnp.sum(lax.all_to_all(spread, FSDP, 0, 0, tiled=True), axis=0)]
    all_to_all x2, starting transfers between devices: 16.9 us -> 15.6 us  [exchanged(): lax.all_to_all(blocks, every, 0, 0, tiled=True, axis_index_groups=groups(...]
    all_to_all x2, waiting for transfers between devices: 1.71 us -> 0.51 us  [exchanged(): lax.all_to_all(blocks, every, 0, 0, tiled=True, axis_index_groups=groups(...]
  transfers between devices with their start and end apart: 6 -> 8, of which waited for: 4 -> 5; matrix products, arithmetic and copies ran while one was open for 6% -> 6% of each run, Pallas kernels for 1% -> 1%
where the time goes in v7:
time: 98.8 us; the launch traced here: 97.9 us
  starting transfers between devices  46.4 us (47%)
  blocking collectives  19.6 us (20%)
  waiting for transfers between devices  14.4 us (15%)
  other arithmetic  8.86 us (9%)
  Pallas kernels  3.96 us (4%)
  between operations  3.56 us (4%)
  local copies, waits for them, and re-layouts  1.27 us (1%)
    ppermute x5, starting transfers between devices, swapped(): return lax.ppermute(value, axis, [(i, i ^ bit) for i in range(size)])  22.8 us
    all_to_all x2, starting transfers between devices, exchanged(): lax.all_to_all(blocks, every, 0, 0, tiled=True, axis_index_groups=groups(...  15.6 us
    all_to_all x1, blocking collectives, line_grad(): lines = lax.all_to_all(spread, ('yh', 'yl'), 0, 0, tiled=True)  14.2 us
    all_to_all x1, waiting for transfers between devices, shards(): checksum = jnp.sum(lax.all_to_all(spread, FSDP, 0, 0, tiled=True), axis=0)  10.5 us
    all_to_all x1, starting transfers between devices, shards(): checksum = jnp.sum(lax.all_to_all(spread, FSDP, 0, 0, tiled=True), axis=0)  7.94 us
    all_gather x1, blocking collectives, line_grad(): return lax.all_gather(jnp.sum(lines, axis=0), 'c', axis=0, tiled=False)  5.4 us
    pallas_call x2, Pallas kernels, turned(): pl.pallas_call(give_kernel if state else turn_kernel, grid_spec=pltpu.Pre...  3.96 us
    ppermute x5, waiting for transfers between devices, swapped(): return lax.ppermute(value, axis, [(i, i ^ bit) for i in range(size)])  3.41 us
  transfers between devices with their start and end apart: 8, of which 5 were waited for; matrix products, arithmetic and copies ran while one was open for 6% of the time, Pallas kernels for 1%

profile of v7, /device:TPU:1, one launch (start us, length us, event | category | flops | bytes accessed | tf_op | source)
XLA Modules:
  0.0 97.9 jit_solution(8894019298724451963)
XLA Ops:
  0.6 2.6 %shard_map.120 = f32[3360,128]{1,0:T(8,128)} custom-call(s32[1]{0:T(128)} %bitcast.4.half_ref, bf16[128,6144]{1,0:T(8,128)(2,1)} %bitcast.89, f32[96,128]{1,0:T(8,128)} %bitcast.98, f32[96,128]{1,0:T(8,128)} %bitcast.95, f32[96,128]{1,0:T(8,128)} %bitcast.92), custom_call_target="tpu_custom_call" | custom-call | bytes 2359296 | tf_op jit(solution)/shard_map/pallas_call | solution.py:100
  3.2 8.8 %collective-permute-start = (f32[3360,128]{1,0:T(8,128)}, f32[3360,128]{1,0:T(8,128)S(1)}, u32[]{:S(2)}, u32[]{:S(2)}) collective-permute-start(f32[3360,128]{1,0:T(8,128)} %shard_map.120), channel_id=1, source_target_pairs={{0,64},{64,0},{1,65},{65,1},{2,66},{66,2},{3,67},{67,3},{4,68},{68... | collective-permute-start | bytes 5160968 | tf_op jit(solution)/shard_map/ppermute | solution.py:23
  12.0 1.4 %shard_map.119 = f32[3072,128]{1,0:T(8,128)S(1)} custom-call(s32[1]{0:T(128)} %bitcast.half_ref, bf16[128,6144]{1,0:T(8,128)(2,1)} %bitcast.90), custom_call_target="tpu_custom_call" | custom-call | bytes 2359296 | tf_op jit(solution)/shard_map/pallas_call | solution.py:100
  14.2 0.6 and_reduce_fusion
  14.8 0.6 fusion.5
  15.5 1.3 %slice_add_fusion = f32[3072,128]{1,0:T(8,128)} fusion(f32[3072,128]{1,0:T(8,128)S(1)} %shard_map.119, f32[3360,128]{1,0:T(8,128)S(1)} %collective-permute-done), kind=kLoop, calls=%fused_computation | loop fusion | flops 393216 | bytes 4718592 | tf_op jit(solution)/shard_map/add | solution.py:123
  16.8 9.2 %all-to-all-start = ((f32[4,768,128]{2,1,0:T(8,128)}), f32[4,768,128]{2,1,0:T(8,128)S(1)}, u32[]{:S(2)}, u32[]{:S(2)}) async-start(f32[4,768,128]{2,1,0:T(8,128)} %bitcast.11), calls=%async_computation | async-start | bytes 3145728 | tf_op jit(solution)/shard_map/all_to_all | solution.py:138
  26.7 0.8 slice_select_fusion
  27.5 3.2 %collective-permute-start.2 = (f32[144,128]{1,0:T(8,128)S(1)}, f32[144,128]{1,0:T(8,128)S(1)}, u32[]{:S(2)}, u32[]{:S(2)}) collective-permute-start(f32[144,128]{1,0:T(8,128)S(1)} %get-tuple-element.49), channel_id=1, source_target_pairs={{0,128},{128,0},{256,384},{384,256},{1,129},{129,1},{257,385},{385... | collective-permute-start | bytes 221192 | tf_op jit(solution)/shard_map/ppermute | solution.py:23
  30.8 4.2 %collective-permute-start.1 = (f32[144,128]{1,0:T(8,128)S(1)}, f32[144,128]{1,0:T(8,128)S(1)}, u32[]{:S(2)}, u32[]{:S(2)}) collective-permute-start(f32[144,128]{1,0:T(8,128)S(1)} %get-tuple-element.50), channel_id=1, source_target_pairs={{0,256},{128,384},{256,0},{384,128},{1,257},{129,385},{257,1},{385... | collective-permute-start | bytes 221192 | tf_op jit(solution)/shard_map/ppermute | solution.py:23
  36.3 1.1 %collective-permute-done.1 = f32[144,128]{1,0:T(8,128)S(1)} collective-permute-done((f32[144,128]{1,0:T(8,128)S(1)}, f32[144,128]{1,0:T(8,128)S(1)}, u32[]{:S(2)}, u32[]{:S(2)}) %collective-permute-start.1) | collective-permute-done | bytes 73760 | tf_op jit(solution)/shard_map/ppermute | solution.py:23
  37.5 0.8 reduce_sum.55
  38.3 6.4 %all-to-all-start.1 = ((f32[8,96,128]{2,1,0:T(8,128)}), f32[8,96,128]{2,1,0:T(8,128)S(1)}, u32[]{:S(2)}, u32[]{:S(2)}) async-start(f32[8,96,128]{2,1,0:T(8,128)} %bitcast.12), calls=%async_computation.1 | async-start | bytes 786432 | tf_op jit(solution)/shard_map/all_to_all | solution.py:138
  44.8 3.2 %collective-permute-start.4 = (f32[144,128]{1,0:T(8,128)S(1)}, f32[144,128]{1,0:T(8,128)S(1)}, u32[]{:S(2)}, u32[]{:S(2)}) collective-permute-start(f32[144,128]{1,0:T(8,128)S(1)} %get-tuple-element.24), channel_id=1, source_target_pairs={{0,256},{128,384},{256,0},{384,128},{1,257},{129,385},{257,1},{385... | collective-permute-start | bytes 221192 | tf_op jit(solution)/shard_map/ppermute | solution.py:23
  48.0 3.4 %collective-permute-start.3 = (f32[144,128]{1,0:T(8,128)S(1)}, f32[144,128]{1,0:T(8,128)S(1)}, u32[]{:S(2)}, u32[]{:S(2)}) collective-permute-start(f32[144,128]{1,0:T(8,128)S(1)} %get-tuple-element.23), channel_id=1, source_target_pairs={{0,128},{128,0},{256,384},{384,256},{1,129},{129,1},{257,385},{385... | collective-permute-start | bytes 221192 | tf_op jit(solution)/shard_map/ppermute | solution.py:23
  51.5 0.7 collective-permute-done.4
  52.2 1.6 %collective-permute-done.3 = f32[144,128]{1,0:T(8,128)S(1)} collective-permute-done((f32[144,128]{1,0:T(8,128)S(1)}, f32[144,128]{1,0:T(8,128)S(1)}, u32[]{:S(2)}, u32[]{:S(2)}) %collective-permute-start.3) | collective-permute-done | bytes 73760 | tf_op jit(solution)/shard_map/ppermute | solution.py:23
  53.7 0.7 fusion
  54.4 0.5 all-to-all-done.1
  55.0 0.1 fusion.6
  55.1 0.1 maximum_bitcast_fusion
  55.5 14.2 %all_to_all.21 = f32[8,48,128]{2,1,0:T(8,128)S(1)} all-to-all(f32[8,48,128]{2,1,0:T(8,128)S(1)} %constant_dynamic-update-slice_fusion), channel_id=1, replica_groups=mesh['yl'=4,'c'=2,'yh'=2,'z'=8,'x'=4] {'yh','yl'}, dimensions={0} | all-to-all | bytes 393216 | tf_op jit(solution)/shard_map/all_to_all | solution.py:148
  69.7 5.4 %all-gather = f32[96,128]{1,0:T(8,128)S(1)} all-gather(f32[48,128]{1,0:T(8,128)S(1)} %reduce_sum.57), channel_id=2, replica_groups=mesh['yl'=4,'c'=2,'yh'=2,'z'=8,'x'=4] {'c'}, dimensions={0}, use_global_device_ids=true | all-gather | bytes 73728 | tf_op jit(solution)/shard_map/all_gather | solution.py:149
  75.5 0.1 broadcast_in_dim.44
  75.6 0.6 broadcast_in_dim.45
  76.2 7.9 %all-to-all-start.3 = ((f32[64,1,128]{2,1,0:T(1,128)}), f32[64,1,128]{2,1,0:T(1,128)S(1)}, u32[]{:S(2)}, u32[]{:S(2)}) async-start(f32[64,1,128]{2,1,0:T(1,128)} %broadcast_in_dim.45), calls=%async_computation.3 | async-start | bytes 65536 | tf_op jit(solution)/shard_map/all_to_all | solution.py:190
  84.1 0.7 fusion.4
  84.9 0.7 maximum_bitcast_fusion.2
  85.6 0.7 maximum_bitcast_fusion.3
  86.3 0.7 convert_bitcast_fusion
  87.0 10.5 %all-to-all-done.3 = f32[64,1,128]{2,1,0:T(1,128)S(1)} async-done(((f32[64,1,128]{2,1,0:T(1,128)}), f32[64,1,128]{2,1,0:T(1,128)S(1)}, u32[]{:S(2)}, u32[]{:S(2)}) %all-to-all-start.3) | async-done | bytes 32800 | tf_op jit(solution)/shard_map/all_to_all | solution.py:190
  97.4 0.5 reduce_sum.59
  (39 shorter events, 0.9 us)
Async XLA Ops:
  3.2 12.3 %collective-permute-start = (f32[3360,128]{1,0:T(8,128)}, f32[3360,128]{1,0:T(8,128)S(1)}, u32[]{:S(2)}, u32[]{:S(2)}) collective-permute-start(f32[3360,128]{1,0:T(8,128)} %shard_map.120), channel_id=1, source_target_pairs={{0,64},{64,0},{1,65},{65,1},{2,66},{66,2},{3,67},{67,3},{4,68},{68... | collective-permute-start | bytes 5160968 | tf_op jit(solution)/shard_map/ppermute | solution.py:23
  12.0 2.2 %copy-start.3 = (s32[8]{0:T(128)S(1)}, s32[8]{0:T(128)}, u32[]{:S(2)}) copy-start(s32[8]{0:T(128)} %param.13) | copy-start | bytes 100
  12.0 2.8 %copy-start.5 = (s32[8]{0:T(128)S(1)}, s32[8]{0:T(128)}, u32[]{:S(2)}) copy-start(s32[8]{0:T(128)} %param.14) | copy-start | bytes 100
  16.8 9.9 %copy-start = (f32[1,128,96]{1,2,0:T(8,128)S(1)}, f32[1,128,96]{1,2,0:T(8,128)}, u32[]{:S(2)}) copy-start(f32[1,128,96]{1,2,0:T(8,128)} %param.11) | copy-start | bytes 147460
  16.8 9.9 %copy-start.1 = (f32[1,128,96]{1,2,0:T(8,128)S(1)}, f32[1,128,96]{1,2,0:T(8,128)}, u32[]{:S(2)}) copy-start(f32[1,128,96]{1,2,0:T(8,128)} %param.10) | copy-start | bytes 147460
  16.8 20.7 %all-to-all-start = ((f32[4,768,128]{2,1,0:T(8,128)}), f32[4,768,128]{2,1,0:T(8,128)S(1)}, u32[]{:S(2)}, u32[]{:S(2)}) async-start(f32[4,768,128]{2,1,0:T(8,128)} %bitcast.11), calls=%async_computation | async-start | bytes 3145728 | tf_op jit(solution)/shard_map/all_to_all | solution.py:138
  27.5 8.8 %collective-permute-start.2 = (f32[144,128]{1,0:T(8,128)S(1)}, f32[144,128]{1,0:T(8,128)S(1)}, u32[]{:S(2)}, u32[]{:S(2)}) collective-permute-start(f32[144,128]{1,0:T(8,128)S(1)} %get-tuple-element.49), channel_id=1, source_target_pairs={{0,128},{128,0},{256,384},{384,256},{1,129},{129,1},{257,385},{385... | collective-permute-start | bytes 221192 | tf_op jit(solution)/shard_map/ppermute | solution.py:23
  30.8 6.7 %collective-permute-start.1 = (f32[144,128]{1,0:T(8,128)S(1)}, f32[144,128]{1,0:T(8,128)S(1)}, u32[]{:S(2)}, u32[]{:S(2)}) collective-permute-start(f32[144,128]{1,0:T(8,128)S(1)} %get-tuple-element.50), channel_id=1, source_target_pairs={{0,256},{128,384},{256,0},{384,128},{1,257},{129,385},{257,1},{385... | collective-permute-start | bytes 221192 | tf_op jit(solution)/shard_map/ppermute | solution.py:23
  36.3 8.4 %copy-start.4 = (f32[96]{0:T(128)S(1)}, f32[96]{0:T(128)}, u32[]{:S(2)}) copy-start(f32[96]{0:T(128)} %param.12) | copy-start | bytes 1156
  36.3 17.5 %copy-start.2 = (f32[1,128,96]{1,2,0:T(8,128)S(1)}, f32[1,128,96]{1,2,0:T(8,128)}, u32[]{:S(2)}) copy-start(f32[1,128,96]{1,2,0:T(8,128)} %param.9) | copy-start | bytes 147460
  38.3 16.6 %all-to-all-start.1 = ((f32[8,96,128]{2,1,0:T(8,128)}), f32[8,96,128]{2,1,0:T(8,128)S(1)}, u32[]{:S(2)}, u32[]{:S(2)}) async-start(f32[8,96,128]{2,1,0:T(8,128)} %bitcast.12), calls=%async_computation.1 | async-start | bytes 786432 | tf_op jit(solution)/shard_map/all_to_all | solution.py:138
  44.8 7.4 %collective-permute-start.4 = (f32[144,128]{1,0:T(8,128)S(1)}, f32[144,128]{1,0:T(8,128)S(1)}, u32[]{:S(2)}, u32[]{:S(2)}) collective-permute-start(f32[144,128]{1,0:T(8,128)S(1)} %get-tuple-element.24), channel_id=1, source_target_pairs={{0,256},{128,384},{256,0},{384,128},{1,257},{129,385},{257,1},{385... | collective-permute-start | bytes 221192 | tf_op jit(solution)/shard_map/ppermute | solution.py:23
  48.0 5.8 %collective-permute-start.3 = (f32[144,128]{1,0:T(8,128)S(1)}, f32[144,128]{1,0:T(8,128)S(1)}, u32[]{:S(2)}, u32[]{:S(2)}) collective-permute-start(f32[144,128]{1,0:T(8,128)S(1)} %get-tuple-element.23), channel_id=1, source_target_pairs={{0,128},{128,0},{256,384},{384,256},{1,129},{129,1},{257,385},{385... | collective-permute-start | bytes 221192 | tf_op jit(solution)/shard_map/ppermute | solution.py:23
  76.2 21.2 %all-to-all-start.3 = ((f32[64,1,128]{2,1,0:T(1,128)}), f32[64,1,128]{2,1,0:T(1,128)S(1)}, u32[]{:S(2)}, u32[]{:S(2)}) async-start(f32[64,1,128]{2,1,0:T(1,128)} %broadcast_in_dim.45), calls=%async_computation.3 | async-start | bytes 65536 | tf_op jit(solution)/shard_map/all_to_all | solution.py:190
